TPU v7x, 256 devices: a whole 4x4x8 slice. The times are simulated.
256 devices in a mesh: seq: 128 (over x, z, y), vocab: 2 (over core).
Axes of the slice: x: 4, y: 4, z: 8, core: 2. Of those that a mesh axis runs over, the one named last changes fastest.
Arguments:
- mamba_in: bfloat16 [32768, 6144], P('seq', 'vocab'), may hold values from -6 to 6
- mamba_gate: bfloat16 [32768, 6144], P('seq', 'vocab'), may hold values from -6 to 6
- conv_weight: float32 [4, 6144], P(None, 'vocab'), may hold values from -0.6 to 0.6
- conv_bias: float32 [6144], P('vocab'), may hold values from -0.5 to 0.5
- x_proj: bfloat16 [6144, 224], P('vocab'), may hold values from -0.078125 to 0.078125
- dt_proj: bfloat16 [192, 6144], P(None, 'vocab'), may hold values from -0.4375 to 0.4375
- dt_bias: float32 [6144], P('vocab'), may hold values from -16 to -4
- a_log: float32 [16, 6144], P(None, 'vocab'), may hold values from 0 to 2.77
- d_skip: float32 [6144], P('vocab'), may hold values from 0.5 to 1.5
- queries: bfloat16 [32768, 3072], P('seq', 'vocab'), may hold values from -6 to 6
- keys: bfloat16 [32768, 384], P('seq', 'vocab'), may hold values from -6 to 6
- att_values: bfloat16 [32768, 384], P('seq', 'vocab'), may hold values from -6 to 6
- logits: bfloat16 [32768, 16384], P('seq', 'vocab'), may hold values from -260 to 260
- targets: int32 [32768], P('seq'), may hold values from 0 to 16383
- allowed: int32 [32768, 2048], P('seq', 'vocab'), may hold values from 0 to 255, as said below
Outputs:
- mamba_out: bfloat16 [32768, 6144], P('seq', 'vocab')
- attention_out: bfloat16 [32768, 3072], P('seq', 'vocab')
- loglik: float32 [32768], P('seq')
Inputs may be any that keep to these rules, and one draw needn't show every extreme that they name: `allowed`: the bit of each token's target is set in its mask.
All inputs are finite; a program needn't handle non-finite values.
Results may differ from a plain program's by a relative error of at most 0.0027.
The roundings to bfloat16 on the way count: a program that leaves them out, or rounds other values in their place, can miss the bound.
Values may be sent and summed in bfloat16 or wider, within the bound.
No kernel may reach another device: no remote copies, remote signals or barrier semaphores. Data moves between devices by JAX's collectives and lax.ppermute only.
A program may use at most 256 MiB of HBM per device.

v0:
```python
import math

import jax
import jax.numpy as jnp
from jax import lax
from jax.sharding import PartitionSpec as P

HEADS = 32
KV_HEADS = 4
HEAD_DIM = 96
WINDOW = 2048


def shifted(value, axis, steps):
    count = lax.axis_size(axis)
    leading, last = (max(0, -steps), min(count, count - steps))
    return lax.ppermute(value, axis, [(source, source + steps) for source in range(leading, last)])


def entering(array, axis, join, neutral):
    place = lax.axis_index(axis)
    gathered = jax.tree.map(
        lambda a, kind: lax.all_gather(a.astype(kind), axis), array, (jnp.bfloat16, jnp.bfloat16)
    )
    state = jax.tree.map(lambda a, e: jnp.zeros_like(a) + jnp.asarray(e, a.dtype), array, neutral)

    def one(step, state):
        return join(
            state,
            jax.tree.map(
                lambda a, own: lax.dynamic_index_in_dim(a, step, 0, False).astype(own.dtype),
                gathered,
                array,
            ),
        )

    return lax.fori_loop(0, place, one, state)


def mamba_part(
    mamba_in, mamba_gate, conv_weight, conv_bias, x_proj, dt_proj, dt_bias, a_log, d_skip
):
    rows, channels = mamba_in.shape
    taps = conv_weight.shape[0]
    rank = dt_proj.shape[0]
    nstate = a_log.shape[0]
    rim = shifted(mamba_in[rows - (taps - 1) :], "seq", 1)
    padded = jnp.concatenate((rim, mamba_in), axis=0).astype(jnp.float32)
    conv = conv_bias[None, :] + conv_weight[0][None, :] * padded[0:rows]
    for tap in range(1, taps):
        conv = conv + conv_weight[tap][None, :] * padded[tap : tap + rows]
    conv_out = jax.nn.silu(conv).astype(jnp.bfloat16)
    partial_proj = jnp.dot(conv_out, x_proj, preferred_element_type=jnp.float32)
    proj = lax.psum(partial_proj, "vocab")
    dt_low = proj[:, :rank].astype(jnp.bfloat16)
    b_all = proj[:, rank : rank + nstate]
    c_all = proj[:, rank + nstate :]
    delta = jax.nn.softplus(
        jnp.dot(dt_low, dt_proj, preferred_element_type=jnp.float32) + dt_bias[None, :]
    )
    a_mat = -jnp.exp(a_log)
    inputs_f = conv_out.astype(jnp.float32)
    unroll = math.gcd(rows, 8)
    count = rows // unroll
    delta_b = delta.reshape(count, unroll, channels)
    inputs_b = inputs_f.reshape(count, unroll, channels)
    b_blocks = b_all.reshape(count, unroll, nstate)
    c_blocks = c_all.reshape(count, unroll, nstate)

    def end_step(state, inputs):
        delta_k, input_k, b_k = inputs
        for inner in range(unroll):
            state = (
                jnp.exp(delta_k[inner][None, :] * a_mat) * state
                + (delta_k[inner] * input_k[inner])[None, :] * b_k[inner][:, None]
            )
        return (state, None)

    def out_step(state, inputs):
        delta_k, input_k, b_k, c_k = inputs
        outputs = []
        for inner in range(unroll):
            state = (
                jnp.exp(delta_k[inner][None, :] * a_mat) * state
                + (delta_k[inner] * input_k[inner])[None, :] * b_k[inner][:, None]
            )
            outputs.append(jnp.sum(c_k[inner][:, None] * state, axis=0))
        return (state, jnp.stack(outputs, axis=0))

    zero_state = jnp.zeros((nstate, channels), jnp.float32)
    state_end, _ = lax.scan(end_step, zero_state, (delta_b, inputs_b, b_blocks))
    summed_end = jnp.sum(delta, axis=0)

    def linear_combine(earlier, later):
        return (earlier[0] * later[0], earlier[1] * later[0] + later[1])

    decay_total = jnp.exp(a_mat * summed_end[None, :])
    identity = (
        jnp.ones((nstate, channels), jnp.float32),
        jnp.zeros((nstate, channels), jnp.float32),
    )
    incoming = entering((decay_total, state_end), "seq", linear_combine, identity)[1]
    _, local_out = lax.scan(out_step, incoming, (delta_b, inputs_b, b_blocks, c_blocks))
    result = local_out.reshape(rows, channels) + d_skip[None, :] * inputs_f
    return (result * jax.nn.silu(mamba_gate.astype(jnp.float32))).astype(jnp.bfloat16)


def attention_part(queries, keys, att_values):
    rows = queries.shape[0]
    kv_width = keys.shape[1]
    groups = HEADS // KV_HEADS
    local_kv = kv_width // HEAD_DIM
    reach = WINDOW // rows
    scale = HEAD_DIM ** (-0.5)
    joined = jnp.concatenate((keys, att_values), axis=1)
    pieces = [shifted(joined, "seq", step) for step in range(reach, 0, -1)]
    buffer = jnp.concatenate(pieces + [joined], axis=0)
    span = buffer.shape[0]
    device = lax.axis_index("seq")
    qpos = jnp.arange(rows, dtype=jnp.int32)[:, None]
    cpos = jnp.arange(span, dtype=jnp.int32)[None, :]
    visible = (cpos > qpos) & (cpos <= reach * rows + qpos) & (cpos >= (reach - device) * rows)
    results = []
    for head in range(local_kv):
        query_head = queries[:, head * groups * HEAD_DIM : (head + 1) * groups * HEAD_DIM].reshape(
            rows, groups, HEAD_DIM
        )
        key_head = buffer[:, head * HEAD_DIM : (head + 1) * HEAD_DIM]
        value_head = buffer[:, kv_width + head * HEAD_DIM : kv_width + (head + 1) * HEAD_DIM]
        score = (
            jnp.einsum("qgd,cd->gqc", query_head, key_head, preferred_element_type=jnp.float32)
            * scale
        )
        score = jnp.where(visible[None], score, -jnp.inf)
        top = jnp.max(score, axis=2, keepdims=True)
        prob = jnp.exp(score - top)
        total = jnp.sum(prob, axis=2)
        mixed = jnp.einsum(
            "gqc,cd->qgd", prob.astype(jnp.bfloat16), value_head, preferred_element_type=jnp.float32
        )
        mixed = mixed / jnp.transpose(total)[:, :, None]
        results.append(mixed.reshape(rows, groups * HEAD_DIM))
    return jnp.concatenate(results, axis=1).astype(jnp.bfloat16)


def scoring_part(logits, targets, allowed):
    rows, width = logits.shape
    logits_f = logits.astype(jnp.float32)
    bits = (
        jnp.right_shift(allowed[:, :, None], jnp.arange(8, dtype=jnp.int32)[None, None, :]) & 1
    ).reshape(rows, width) == 1
    masked = jnp.where(bits, logits_f, -jnp.inf)
    local_target = targets - lax.axis_index("vocab") * width
    target_part = jnp.sum(
        jnp.where(
            jnp.arange(width, dtype=jnp.int32)[None, :] == local_target[:, None], logits_f, 0.0
        ),
        axis=1,
    )
    local_top = jnp.max(masked, axis=1)
    top = lax.pmax(local_top, "vocab")
    part_sum = jnp.sum(jnp.exp(masked - top[:, None]), axis=1)
    total, target_logit = lax.psum((part_sum, target_part), "vocab")
    return target_logit - top - jnp.log(total)


def local(
    mamba_in,
    mamba_gate,
    conv_weight,
    conv_bias,
    x_proj,
    dt_proj,
    dt_bias,
    a_log,
    d_skip,
    queries,
    keys,
    att_values,
    logits,
    targets,
    allowed,
):
    mamba_out = mamba_part(
        mamba_in, mamba_gate, conv_weight, conv_bias, x_proj, dt_proj, dt_bias, a_log, d_skip
    )
    attention_out = attention_part(queries, keys, att_values)
    loglik = scoring_part(logits, targets, allowed)
    return (mamba_out, attention_out, loglik)


def solution(mesh):
    in_specs = (
        P("seq", "vocab"),
        P("seq", "vocab"),
        P(None, "vocab"),
        P("vocab"),
        P("vocab", None),
        P(None, "vocab"),
        P("vocab"),
        P(None, "vocab"),
        P("vocab"),
        P("seq", "vocab"),
        P("seq", "vocab"),
        P("seq", "vocab"),
        P("seq", "vocab"),
        P("seq"),
        P("seq", "vocab"),
    )
    out_specs = (P("seq", "vocab"), P("seq", "vocab"), P("seq"))
    return jax.shard_map(local, mesh=mesh, in_specs=in_specs, out_specs=out_specs, check_vma=False)
```

profile of v0, /device:TPU:254, one launch (start us, length us, event | category | flops | bytes accessed | tf_op | source)
XLA Modules:
  0.0 720.2 jit_solution(2034888485994005577)
XLA Ops:
  10.5 3.4 collective-permute-done
  15.7 3.3 convert_bitcast_fusion
  20.5 29.8 %all-reduce.3.cloned.1.call-done = f32[256,224]{0,1:T(8,128)} async-done(((f32[256,224]{0,1:T(8,128)}), f32[256,224]{0,1:T(8,128)}) %all-reduce.3.cloned.1.call-update) | async-done | bytes 229392 | tf_op jit(solution)/shard_map/psum | solution.py:54
  51.1 5.2 fusion.73
  57.1 82.5 %while.37 = (s32[]{:T(128)}, f32[16,3072]{1,0:T(8,128)S(1)}, f32[32,8,3072]{2,1,0:T(8,128)}, f32[16,3072]{1,0:T(8,128)S(1)}, f32[32,8,3072]{2,1,0:T(8,128)}, /*i...) while((s32[]{:T(128)}, f32[16,3072]{1,0:T(8,128)S(1)}, ...), condition=%wide.region_3.4_spmd.clone, body=%wide.region_2.3_spmd.clone.sunk | while | flops 1646602 | bytes 1477391 | solution.py:91
  62.0 2.0 constant_dynamic-slice_fusion.42
  69.5 2.3 constant_dynamic-slice_fusion.42
  74.6 2.5 constant_dynamic-slice_fusion.42
  77.6 2.0 constant_dynamic-slice_fusion.42
  82.6 2.2 constant_dynamic-slice_fusion.42
  85.3 2.0 constant_dynamic-slice_fusion.42
  87.8 2.2 constant_dynamic-slice_fusion.42
  95.4 2.2 constant_dynamic-slice_fusion.42
  98.2 2.0 constant_dynamic-slice_fusion.42
  105.7 2.2 constant_dynamic-slice_fusion.42
  115.8 2.0 constant_dynamic-slice_fusion.42
  118.3 2.2 constant_dynamic-slice_fusion.42
  123.5 2.5 constant_dynamic-slice_fusion.42
  131.5 2.3 constant_dynamic-slice_fusion.42
  134.3 2.3 constant_dynamic-slice_fusion.42
  148.8 6.4 copy.35
  157.1 7.0 fusion.28
  164.2 2.5 pmax.7
  166.6 6.7 fusion.31
  173.4 2.5 all-reduce
  190.5 2.4 collective-permute-done.6
  192.9 6.0 collective-permute-done.7
  199.7 8.2 %fusion.19 = (f32[8,256]{1,0:T(8,128)S(1)}, f32[2304,256,8]{1,0,2:T(8,128)}) fusion(pred[256,2304]{0,1:T(8,128)(4,1)S(1)} %fusion.45, bf16[256,8,96]{0,2,1:T(8,128)(2,1)S(1)} %bitcast.318, bf16[2304,384]{0,1:T(8,128)(2,1)S(1)} %constant_dynamic-update-slice_fusion.11), kind=kOutput, calls=%fused_computation.102 | convolution fusion | flops 920123392 | bytes 20307968 | tf_op jit(solution)/shard_map/qgd,cd->gqc/dot_general | solution.py:131
  207.9 17.8 %fusion.15 = (f32[8,256]{1,0:T(8,128)S(1)}, f32[8,256]{1,0:T(8,128)S(1)}, f32[2304,256,8]{1,0,2:T(8,128)}) fusion(f32[2304,256,8]{1,0,2:T(8,128)} %get-tuple-element.302, f32[8,256]{1,0:T(8,128)S(1)} %get-tuple-element.301, pred[256,2304]{0,1:T(8,128)(4,1)S(1)} %fusion.45, bf16[256,8,96]{0,2,1:T(8,128)(2,1)S(1)} %bitcast.343, ...), kind=kOutput, calls=%fused_computation.98 | convolution fusion | flops 938995712 | bytes 39198720 | tf_op jit(solution)/shard_map/qgd,cd->gqc/dot_general | solution.py:131
  225.7 9.1 %fusion.61 = bf16[256,8,96]{0,2,1:T(8,128)(2,1)S(1)} fusion(f32[2304,256,8]{1,0,2:T(8,128)} %get-tuple-element.302, f32[8,256]{1,0:T(8,128)S(1)} %get-tuple-element.301, pred[256,2304]{0,1:T(8,128)(4,1)S(1)} %fusion.45, bf16[2304,384]{0,1:T(8,128)(2,1)S(1)} %constant_dynamic-update-slice_fusion.11, f32[256,8]{0,1:T(8,128)S(1)} %bitcast.356), kind=kOutput, calls=%fused_computation.150 | convolution fusion | flops 925237248 | bytes 20316160 | tf_op jit(solution)/shard_map/gqc,cd->qgd/dot_general | solution.py:138
  235.0 10.2 %fusion.17 = f32[8,256]{1,0:T(8,128)S(1)} fusion(f32[2304,256,8]{1,0,2:T(8,128)} %get-tuple-element.303, f32[8,256]{1,0:T(8,128)S(1)} %get-tuple-element.169, pred[256,2304]{0,1:T(8,128)(4,1)S(1)} %fusion.45), kind=kLoop, calls=%fused_computation.100 | loop fusion | flops 18872320 | bytes 19480576 | tf_op jit(solution)/shard_map/reduce_sum | solution.py:137
  245.2 12.0 %fusion.55 = bf16[256,8,96]{0,2,1:T(8,128)(2,1)S(1)} fusion(f32[2304,256,8]{1,0,2:T(8,128)} %get-tuple-element.303, f32[8,256]{1,0:T(8,128)S(1)} %get-tuple-element.169, pred[256,2304]{0,1:T(8,128)(4,1)S(1)} %fusion.45, bf16[2304,384]{0,1:T(8,128)(2,1)} %copy-done.6, f32[256,8]{0,1:T(8,128)S(1)} %bitcast.355), kind=kOutput, calls=%fused_computation.148 | convolution fusion | flops 925237248 | bytes 20316160 | tf_op jit(solution)/shard_map/gqc,cd->qgd/dot_general | solution.py:138
  258.4 33.0 %all-gather.7.cloned.1.call-done = bf16[2048,3072]{1,0:T(8,128)(2,1)} async-done(((bf16[16,3072]{1,0:T(8,128)(2,1)}), bf16[2048,3072]{1,0:T(8,128)(2,1)}) %all-gather.7.cloned.1.call-update) | async-done | bytes 12582928 | tf_op jit(solution)/shard_map/all_gather | solution.py:23
  291.4 136.9 %all-gather.5.cloned.1.call-done = bf16[2048,3072]{1,0:T(8,128)(2,1)} async-done(((bf16[16,3072]{1,0:T(8,128)(2,1)}), bf16[2048,3072]{1,0:T(8,128)(2,1)}) %all-gather.5.cloned.1.call-update) | async-done | bytes 12582928 | tf_op jit(solution)/shard_map/all_gather | solution.py:23
  428.3 132.1 %while.35 = (s32[]{:T(128)}, f32[16,3072]{1,0:T(8,128)S(1)}, s32[]{:T(128)}, bf16[128,16,3072]{2,1,0:T(8,128)(2,1)}, bf16[128,16,3072]{2,1,0:T(8,128)(2,1)}, /*index=5*/s32[]{:T(128)}, s32[]{:T(128)}, s32[]{:T(128)}) while((s32[]{:T(128)}, f32[16,3072]{1,0:T(8,128)S(1)}, s32[]{:T(128)}, bf16[128,16,3072]{2,1,0:T(8,128)(2,1)}, ...), condition=%wide.region_5.6_spmd, body=%wide.region_4.5_spmd.sunk | while | flops 196613 | bytes 589947 | solution.py:37
  560.4 148.5 %while.36 = (s32[]{:T(128)}, f32[16,3072]{1,0:T(8,128)S(1)}, f32[32,8,3072]{2,1,0:T(8,128)}, f32[32,8,3072]{2,1,0:T(8,128)}, f32[16,3072]{1,0:T(8,128)S(1)}, /*i...) while((s32[]{:T(128)}, f32[16,3072]{1,0:T(8,128)S(1)}, ...), condition=%wide.region_15.16_spmd, body=%wide.region_6.15_spmd.sunk | while | flops 3538953 | bytes 3102869 | solution.py:103
  583.2 2.3 constant_dynamic-slice_fusion.40
  592.4 2.5 constant_dynamic-slice_fusion.40
  606.6 2.2 constant_dynamic-slice_fusion.40
  615.9 2.2 constant_dynamic-slice_fusion.40
  629.7 2.2 constant_dynamic-slice_fusion.40
  648.2 2.2 constant_dynamic-slice_fusion.40
  666.6 2.0 constant_dynamic-slice_fusion.40
  671.2 2.2 constant_dynamic-slice_fusion.40
  680.5 2.5 constant_dynamic-slice_fusion.40
  694.6 2.2 constant_dynamic-slice_fusion.40
  699.5 2.3 constant_dynamic-slice_fusion.40
  708.9 4.7 fusion.36
  (1114 shorter events, 332.5 us)
Async XLA Ops:
  7.2 11.9 %copy-start = (bf16[3072,224]{0,1:T(8,128)(2,1)S(1)}, bf16[3072,224]{0,1:T(8,128)(2,1)}, u32[]{:S(2)}) copy-start(bf16[3072,224]{0,1:T(8,128)(2,1)} %param.25) | copy-start | bytes 4128772
  7.2 8.6 %copy-start.9 = (f32[3072]{0:T(1024)S(1)}, f32[3072]{0:T(1024)}, u32[]{:S(2)}) copy-start(f32[3072]{0:T(1024)} %param.24) | copy-start | bytes 36868
  7.2 43.1 %all-reduce.3.cloned.1.call-start = ((), (), s32[]{:S(2)}) async-start(), calls=%async_computation | async-start | bytes 458752 | tf_op jit(solution)/shard_map/psum | solution.py:54
  8.2 5.7 collective-permute-start
  19.0 32.1 %copy-start.12 = (f32[3072]{0:T(1024)S(1)}, f32[3072]{0:T(1024)}, u32[]{:S(2)}) copy-start(f32[3072]{0:T(1024)} %param.27) | copy-start | bytes 36868
  20.4 271.0 %all-gather.7.cloned.1.call-start = ((), (), s32[]{:S(2)}) async-start(), calls=%async_computation.2 | async-start | bytes 12681216 | tf_op jit(solution)/shard_map/all_gather | solution.py:23
  51.1 5.3 copy-start.8
  57.1 84.0 %copy-start.3 = (bf16[256,192]{0,1:T(8,128)(2,1)S(1)}, bf16[256,192]{0,1:T(8,128)(2,1)}, u32[]{:S(2)}) copy-start(bf16[256,192]{0,1:T(8,128)(2,1)} %param.31) | copy-start | bytes 294916
  57.1 84.6 %copy-start.4 = (bf16[256,192]{0,1:T(8,128)(2,1)S(1)}, bf16[256,192]{0,1:T(8,128)(2,1)}, u32[]{:S(2)}) copy-start(bf16[256,192]{0,1:T(8,128)(2,1)} %param.32) | copy-start | bytes 294916
  139.6 9.3 %copy-start.7 = (f32[32,8,16]{2,1,0:T(8,128)}, f32[32,8,16]{2,1,0:T(8,128)S(1)}, u32[]{:S(2)}) copy-start(f32[32,8,16]{2,1,0:T(8,128)S(1)} %get-tuple-element.690) | copy-start | bytes 49156
  140.3 288.0 %all-gather.5.cloned.1.call-start = ((), (), s32[]{:S(2)}) async-start(), calls=%async_computation.1 | async-start | bytes 12681216 | tf_op jit(solution)/shard_map/all_gather | solution.py:23
  142.3 39.3 %collective-permute-start.1 = (bf16[256,384]{0,1:T(8,128)(2,1)}, bf16[256,384]{0,1:T(8,128)(2,1)}, u32[]{:S(2)}, u32[]{:S(2)}) collective-permute-start(bf16[256,384]{0,1:T(8,128)(2,1)} %constant_dynamic-update-slice_fusion), channel_id=1, source_target_pairs={{0,16},{2,18},{4,20},{6,22},{8,24},{10,26},{12,28},{14,30},{16,32}... | collective-permute-start | bytes 589832 | tf_op jit(solution)/shard_map/ppermute | solution.py:17
  143.6 40.3 %collective-permute-start.2 = (bf16[256,384]{0,1:T(8,128)(2,1)}, bf16[256,384]{0,1:T(8,128)(2,1)}, u32[]{:S(2)}, u32[]{:S(2)}) collective-permute-start(bf16[256,384]{0,1:T(8,128)(2,1)} %constant_dynamic-update-slice_fusion), channel_id=1, source_target_pairs={{0,14},{2,16},{4,18},{6,20},{8,22},{10,24},{12,26},{14,28},{16,30}... | collective-permute-start | bytes 589832 | tf_op jit(solution)/shard_map/ppermute | solution.py:17
  144.9 41.2 %collective-permute-start.3 = (bf16[256,384]{0,1:T(8,128)(2,1)}, bf16[256,384]{0,1:T(8,128)(2,1)}, u32[]{:S(2)}, u32[]{:S(2)}) collective-permute-start(bf16[256,384]{0,1:T(8,128)(2,1)} %constant_dynamic-update-slice_fusion), channel_id=1, source_target_pairs={{0,12},{2,14},{4,16},{6,18},{8,20},{10,22},{12,24},{14,26},{16,28}... | collective-permute-start | bytes 589832 | tf_op jit(solution)/shard_map/ppermute | solution.py:17
  146.2 42.4 %collective-permute-start.4 = (bf16[256,384]{0,1:T(8,128)(2,1)}, bf16[256,384]{0,1:T(8,128)(2,1)}, u32[]{:S(2)}, u32[]{:S(2)}) collective-permute-start(bf16[256,384]{0,1:T(8,128)(2,1)} %constant_dynamic-update-slice_fusion), channel_id=1, source_target_pairs={{0,10},{2,12},{4,14},{6,16},{8,18},{10,20},{12,22},{14,24},{16,26}... | collective-permute-start | bytes 589832 | tf_op jit(solution)/shard_map/ppermute | solution.py:17
  147.5 42.0 %collective-permute-start.5 = (bf16[256,384]{0,1:T(8,128)(2,1)}, bf16[256,384]{0,1:T(8,128)(2,1)}, u32[]{:S(2)}, u32[]{:S(2)}) collective-permute-start(bf16[256,384]{0,1:T(8,128)(2,1)} %constant_dynamic-update-slice_fusion), channel_id=1, source_target_pairs={{0,8},{2,10},{4,12},{6,14},{8,16},{10,18},{12,20},{14,22},{16,24},... | collective-permute-start | bytes 589832 | tf_op jit(solution)/shard_map/ppermute | solution.py:17
  156.8 9.8 %copy-start.11 = (s32[256]{0:T(256)S(1)}, s32[256]{0:T(256)}, u32[]{:S(2)}) copy-start(s32[256]{0:T(256)} %param.34) | copy-start | bytes 3076
  177.7 21.9 %copy-start.5 = (bf16[256,192]{0,1:T(8,128)(2,1)S(1)}, bf16[256,192]{0,1:T(8,128)(2,1)}, u32[]{:S(2)}) copy-start(bf16[256,192]{0,1:T(8,128)(2,1)} %param.32) | copy-start | bytes 294916
  181.7 11.2 %collective-permute-start.6 = (bf16[256,384]{0,1:T(8,128)(2,1)}, bf16[256,384]{0,1:T(8,128)(2,1)S(1)}, u32[]{:S(2)}, u32[]{:S(2)}) collective-permute-start(bf16[256,384]{0,1:T(8,128)(2,1)} %constant_dynamic-update-slice_fusion), channel_id=1, source_target_pairs={{0,6},{2,8},{4,10},{6,12},{8,14},{10,16},{12,18},{14,20},{16,22},{... | collective-permute-start | bytes 589832 | tf_op jit(solution)/shard_map/ppermute | solution.py:17
  183.9 14.9 %collective-permute-start.7 = (bf16[256,384]{0,1:T(8,128)(2,1)}, bf16[256,384]{0,1:T(8,128)(2,1)S(1)}, u32[]{:S(2)}, u32[]{:S(2)}) collective-permute-start(bf16[256,384]{0,1:T(8,128)(2,1)} %constant_dynamic-update-slice_fusion), channel_id=1, source_target_pairs={{0,4},{2,6},{4,8},{6,10},{8,12},{10,14},{12,16},{14,18},{16,20},{1... | collective-permute-start | bytes 589832 | tf_op jit(solution)/shard_map/ppermute | solution.py:17
  186.2 13.4 %collective-permute-start.8 = (bf16[256,384]{0,1:T(8,128)(2,1)}, bf16[256,384]{0,1:T(8,128)(2,1)S(1)}, u32[]{:S(2)}, u32[]{:S(2)}) collective-permute-start(bf16[256,384]{0,1:T(8,128)(2,1)} %constant_dynamic-update-slice_fusion), channel_id=1, source_target_pairs={{0,2},{2,4},{4,6},{6,8},{8,10},{10,12},{12,14},{14,16},{16,18},{18... | collective-permute-start | bytes 589832 | tf_op jit(solution)/shard_map/ppermute | solution.py:17
  199.7 26.1 %copy-start.6 = (bf16[2304,384]{0,1:T(8,128)(2,1)}, bf16[2304,384]{0,1:T(8,128)(2,1)S(1)}, u32[]{:S(2)}) copy-start(bf16[2304,384]{0,1:T(8,128)(2,1)S(1)} %constant_dynamic-update-slice_fusion.11) | copy-start | bytes 5308420
  199.7 8.2 %copy-start.2 = (bf16[256,768]{0,1:T(8,128)(2,1)S(1)}, bf16[256,768]{0,1:T(8,128)(2,1)}, u32[]{:S(2)}) copy-start(bf16[256,768]{0,1:T(8,128)(2,1)} %copy.31) | copy-start | bytes 1179652
  560.4 148.6 %copy-start.10 = (f32[3072]{0:T(1024)S(1)}, f32[3072]{0:T(1024)}, u32[]{:S(2)}) copy-start(f32[3072]{0:T(1024)} %param.29) | copy-start | bytes 36868
  708.9 4.7 copy-start.1
Sparse Core Ops, SparseCore 0:
  20.5 29.6 all-reduce.2
  140.4 150.9 all-gather.6
  295.1 133.1 all-gather.4
where the time goes:
time: 730 us; the launch traced here: 720 us
  waiting for transfers between devices  213 us (29%)
  other arithmetic  212 us (29%)
  local copies, waits for them, and re-layouts  201 us (28%)
  matrix products  53.7 us (7%)
  between operations  14.1 us (2%)
  starting transfers between devices  11.9 us (2%)
  loops' own time  9.11 us (1%)
    all_gather x2, waiting for transfers between devices, entering(): lax.all_gather(a.astype(kind), axis)  170 us
    add x127, other arithmetic, linear_combine(): return (earlier[0] * later[0], earlier[1] * later[0] + later[1])  129 us
    slice x32, local copies, waits for them, and re-layouts, end_step(): input_k[inner]  65.9 us
    slice x32, local copies, waits for them, and re-layouts, out_step(): input_k[inner]  65.3 us
    reduce_sum x96, other arithmetic, out_step(): outputs.append(jnp.sum(c_k[inner][:, None] * state, axis=0))  31.3 us
    psum x1, waiting for transfers between devices, mamba_part(): proj = lax.psum(partial_proj, 'vocab')  29.8 us
    dot_general x2, matrix products, attention_part(): jnp.einsum('qgd,cd->gqc', query_head, key_head, preferred_element_type=jn...  26 us
    dynamic_slice x64, local copies, waits for them, and re-layouts, mamba_part(): state_end, _ = lax.scan(end_step, zero_state, (delta_b, inputs_b, b_blocks))  22.3 us
  transfers between devices with their start and end apart: 12, of which 7 were waited for; matrix products, arithmetic and copies ran while one was open for 13% of the time, Pallas kernels for 0%

commit v1 on v0

v1 whole, which is shorter than its diff:
```python
import jax
import jax.numpy as jnp
from jax import lax
from jax.experimental import pallas as pl
from jax.experimental.pallas import tpu as pltpu
from jax.sharding import PartitionSpec as P

HEADS = 32
KV_HEADS = 4
HEAD_DIM = 96
WINDOW = 2048
LOG2E = 1.4426950408889634
F32 = jnp.float32
BF16 = jnp.bfloat16
GROUP = 1024
LANES = 128
LOW = -1e30


def params(mib):
    return pltpu.CompilerParams(vmem_limit_bytes=mib * 1024 * 1024)


def cost(flops, nbytes, trans=0):
    return pl.CostEstimate(flops=int(flops), bytes_accessed=int(nbytes), transcendentals=int(trans))


def shifted(value, axis, steps):
    count = lax.axis_size(axis)
    leading, last = (max(0, -steps), min(count, count - steps))
    return lax.ppermute(value, axis, [(source, source + steps) for source in range(leading, last)])


def swapped(value):
    return lax.ppermute(value, "vocab", [(0, 1), (1, 0)])


def score_kernel(logits_ref, allowed_ref, local_target_ref, out_ref):
    rows, width = logits_ref.shape
    words = LANES
    span = words * 8
    row_id = lax.broadcasted_iota(jnp.int32, (words, span), 0)
    col_id = lax.broadcasted_iota(jnp.int32, (words, span), 1)
    expand = jnp.where(row_id == col_id // 8, 1.0, 0.0).astype(BF16)
    col = lax.broadcasted_iota(jnp.int32, (rows, span), 1)
    bit = jnp.left_shift(jnp.int32(1), col & 7)
    wanted = local_target_ref[...]
    top = jnp.full((rows, LANES), -jnp.inf, F32)
    target = jnp.zeros((rows, LANES), F32)
    parts = []
    for block in range(width // span):
        values = logits_ref[:, block * span : (block + 1) * span].astype(F32)
        word = allowed_ref[:, block * words : (block + 1) * words].astype(F32).astype(BF16)
        spread = jnp.dot(word, expand, preferred_element_type=F32).astype(jnp.int32)
        masked = jnp.where((spread & bit) != 0, values, -jnp.inf)
        hit = jnp.where(col == wanted - block * span, values, 0.0)
        for piece in range(8):
            at = slice(piece * LANES, (piece + 1) * LANES)
            top = jnp.maximum(top, masked[:, at])
            target = target + hit[:, at]
        parts.append(masked)
    best = jnp.maximum(jnp.max(top, axis=1, keepdims=True), LOW)
    total = jnp.zeros((rows, LANES), F32)
    for masked in parts:
        terms = jnp.exp(masked - best)
        for piece in range(8):
            total = total + terms[:, piece * LANES : (piece + 1) * LANES]
    summed = jnp.sum(total, axis=1, keepdims=True)
    found = jnp.sum(target, axis=1, keepdims=True)
    lane = lax.broadcasted_iota(jnp.int32, (rows, LANES), 1)
    out_ref[...] = jnp.where(lane == 0, best, jnp.where(lane == 1, summed, found))


def scoring_part(logits, targets, allowed):
    rows, width = logits.shape
    block = 32
    local_target = (targets - lax.axis_index("vocab") * width).reshape(rows, 1)
    stats = pl.pallas_call(
        score_kernel,
        grid=(rows // block,),
        in_specs=[
            pl.BlockSpec((block, width), lambda i: (i, 0)),
            pl.BlockSpec((block, width // 8), lambda i: (i, 0)),
            pl.BlockSpec((block, 1), lambda i: (i, 0)),
        ],
        out_specs=pl.BlockSpec((block, LANES), lambda i: (i, 0)),
        out_shape=jax.ShapeDtypeStruct((rows, LANES), F32),
        compiler_params=params(48),
        cost_estimate=cost(rows * width * 256, rows * width * 3, rows * width),
        name="scoring",
    )(logits, allowed, local_target)
    return stats[:, :8].T


def scoring_join(mine, other):
    top = jnp.maximum(mine[0], other[0])
    total = mine[1] * jnp.exp(mine[0] - top) + other[1] * jnp.exp(other[0] - top)
    return mine[2] + other[2] - top - jnp.log(total)


def conv_kernel(x_ref, rim_ref, weight_ref, bias_ref, proj_ref, conv_ref, out_ref, pad):
    rows = x_ref.shape[0]
    taps = weight_ref.shape[0]
    x = x_ref[...].astype(F32)
    pad[8 : 8 + rows, :] = x
    pad[8 - (taps - 1) : 8, :] = rim_ref[...].astype(F32)
    conv = bias_ref[...]
    for tap in range(taps):
        start = 8 - (taps - 1) + tap
        conv = conv + weight_ref[tap : tap + 1, :] * pad[start : start + rows, :]
    value = (conv / (1.0 + jnp.exp(-conv))).astype(BF16)
    conv_ref[...] = value
    part = jnp.dot(value, proj_ref[...], preferred_element_type=F32)

    @pl.when(pl.program_id(0) == 0)
    def _():
        out_ref[...] = part

    @pl.when(pl.program_id(0) > 0)
    def _():
        out_ref[...] += part


def convolve(mamba_in, rim, conv_weight, conv_bias, x_proj):
    rows, channels = mamba_in.shape
    taps = conv_weight.shape[0]
    width = x_proj.shape[1]
    block = 512
    return pl.pallas_call(
        conv_kernel,
        grid=(channels // block,),
        in_specs=[
            pl.BlockSpec((rows, block), lambda i: (0, i)),
            pl.BlockSpec((taps - 1, block), lambda i: (0, i)),
            pl.BlockSpec((taps, block), lambda i: (0, i)),
            pl.BlockSpec((1, block), lambda i: (0, i)),
            pl.BlockSpec((block, width), lambda i: (i, 0)),
        ],
        out_specs=[
            pl.BlockSpec((rows, block), lambda i: (0, i)),
            pl.BlockSpec((rows, width), lambda i: (0, 0)),
        ],
        out_shape=[
            jax.ShapeDtypeStruct((rows, channels), BF16),
            jax.ShapeDtypeStruct((rows, width), F32),
        ],
        scratch_shapes=[pltpu.VMEM((rows + 8, block), F32)],
        compiler_params=params(32),
        cost_estimate=cost(rows * channels * 700, rows * channels * 4, rows * channels * 2),
        name="convolution",
    )(mamba_in, rim, conv_weight, conv_bias.reshape(1, channels), x_proj)


def softplus(v):
    e = jnp.exp(-jnp.abs(v))
    return jnp.maximum(v, 0.0) + jnp.log1p(e)


def scan_kernel(
    low_ref, dt_ref, bias_ref, alog_ref, skip_ref, conv_ref, b_ref, c_ref,
    y_ref, cum_ref, end_ref, delta_s, x_s,
):
    rows = low_ref.shape[0]
    nstate = alog_ref.shape[0]
    delta = softplus(jnp.dot(low_ref[...], dt_ref[...], preferred_element_type=F32) + bias_ref[...])
    x = conv_ref[...].astype(F32)
    for sub in range(8):
        at = slice(sub * LANES, (sub + 1) * LANES)
        delta_s[:, sub, :] = delta[:, at]
        x_s[:, sub, :] = x[:, at]
    rate = [-LOG2E * jnp.exp(alog_ref[n]) for n in range(nstate)]
    skip = skip_ref[...]

    def step(t, carry):
        cum, state = carry
        d = delta_s[t]
        x_t = x_s[t]
        cum = cum + d
        dx = d * x_t
        y = skip * x_t
        new = []
        for n in range(nstate):
            row = t * nstate + n
            h = jnp.exp2(d * rate[n]) * state[n] + dx * b_ref[pl.ds(row, 1), :]
            y = y + h * c_ref[pl.ds(row, 1), :]
            new.append(h)
        cum_ref[t] = cum
        y_ref[t] = y
        return cum, tuple(new)

    zero = jnp.zeros((8, LANES), F32)
    _, state = lax.fori_loop(0, rows, step, (zero, (zero,) * nstate), unroll=4)
    for n in range(nstate):
        end_ref[n] = state[n]


def local_scan(dt_low, dt_proj, dt_bias, a_log, d_skip, conv_out, b_wide, c_wide):
    rows, channels = conv_out.shape
    rank = dt_low.shape[1]
    nstate = a_log.shape[0]
    subs = channels // LANES
    wide = pl.BlockSpec((rows * nstate, LANES), lambda i: (0, 0))
    folded = pl.BlockSpec((rows, 8, LANES), lambda i: (0, i, 0))
    states = pl.BlockSpec((nstate, 8, LANES), lambda i: (0, i, 0))
    return pl.pallas_call(
        scan_kernel,
        grid=(channels // GROUP,),
        in_specs=[
            pl.BlockSpec((rows, rank), lambda i: (0, 0)),
            pl.BlockSpec((rank, GROUP), lambda i: (0, i)),
            pl.BlockSpec((1, GROUP), lambda i: (0, i)),
            states,
            pl.BlockSpec((8, LANES), lambda i: (i, 0)),
            pl.BlockSpec((rows, GROUP), lambda i: (0, i)),
            wide,
            wide,
        ],
        out_specs=[folded, folded, states],
        out_shape=[
            jax.ShapeDtypeStruct((rows, subs, LANES), F32),
            jax.ShapeDtypeStruct((rows, subs, LANES), F32),
            jax.ShapeDtypeStruct((nstate, subs, LANES), F32),
        ],
        scratch_shapes=[pltpu.VMEM((rows, 8, LANES), F32), pltpu.VMEM((rows, 8, LANES), F32)],
        compiler_params=params(48),
        cost_estimate=cost(rows * channels * nstate * 500, rows * channels * 12, rows * channels * nstate),
        name="local_scan",
    )(
        dt_low, dt_proj, dt_bias.reshape(1, channels), a_log, d_skip.reshape(subs, LANES),
        conv_out, b_wide, c_wide,
    )


def finish_kernel(y_ref, cum_ref, c_ref, state_ref, alog_ref, gate_ref, out_ref, y_s):
    rows = y_ref.shape[0]
    nstate = alog_ref.shape[0]
    rate = [-LOG2E * jnp.exp(alog_ref[n]) for n in range(nstate)]
    state = [state_ref[n] for n in range(nstate)]

    def step(t, carry):
        cum = cum_ref[t]
        y = y_ref[t]
        for n in range(nstate):
            y = y + (jnp.exp2(cum * rate[n]) * state[n]) * c_ref[pl.ds(t * nstate + n, 1), :]
        y_s[t] = y
        return carry

    lax.fori_loop(0, rows, step, 0, unroll=4)
    for sub in range(8):
        at = slice(sub * LANES, (sub + 1) * LANES)
        gate = gate_ref[:, at].astype(F32)
        out_ref[:, at] = (y_s[:, sub, :] * (gate / (1.0 + jnp.exp(-gate)))).astype(BF16)


def finish(y, cum, c_wide, incoming, a_log, mamba_gate):
    rows, channels = mamba_gate.shape
    nstate = a_log.shape[0]
    folded = pl.BlockSpec((rows, 8, LANES), lambda i: (0, i, 0))
    states = pl.BlockSpec((nstate, 8, LANES), lambda i: (0, i, 0))
    return pl.pallas_call(
        finish_kernel,
        grid=(channels // GROUP,),
        in_specs=[
            folded,
            folded,
            pl.BlockSpec((rows * nstate, LANES), lambda i: (0, 0)),
            states,
            states,
            pl.BlockSpec((rows, GROUP), lambda i: (0, i)),
        ],
        out_specs=pl.BlockSpec((rows, GROUP), lambda i: (0, i)),
        out_shape=jax.ShapeDtypeStruct((rows, channels), BF16),
        scratch_shapes=[pltpu.VMEM((rows, 8, LANES), F32)],
        compiler_params=params(48),
        cost_estimate=cost(rows * channels * nstate * 300, rows * channels * 12, rows * channels * nstate),
        name="finish",
    )(y, cum, c_wide, incoming, a_log, mamba_gate)


def entering(summed, state, rate):
    nstate = state.shape[0]
    place = lax.axis_index("seq")
    count = lax.axis_size("seq")

    def join(earlier, later):
        return (earlier[0] + later[0], earlier[1] * jnp.exp(rate * later[0][None]) + later[1])

    def packed(pair):
        high = pair[0].astype(BF16)
        low = (pair[0] - high.astype(F32)).astype(BF16)
        return jnp.concatenate((pair[1].astype(BF16), high[None], low[None]), axis=0)

    def opened(message):
        wide = message.astype(F32)
        return (wide[nstate] + wide[nstate + 1], wide[:nstate])

    total = (summed, state)
    before = None
    stride = 1
    for size in (4, 2, 4, 4):
        message = packed(total)
        mine = (place // stride) % size
        came = [message]
        for k in range(1, size):
            pairs = [(i, i ^ (k * stride)) for i in range(count)]
            came.append(lax.ppermute(message, "seq", pairs))
        ordered = []
        for j in range(size):
            pick = mine ^ j
            chosen = came[0]
            for k in range(1, size):
                chosen = jnp.where(pick == k, came[k], chosen)
            ordered.append(opened(chosen))
        prefix = (jnp.zeros_like(summed), jnp.zeros_like(state))
        running = None
        for j in range(size):
            running = ordered[j] if running is None else join(running, ordered[j])
            if j < size - 1:
                prefix = tuple(jnp.where(mine == j + 1, r, p) for r, p in zip(running, prefix))
        before = prefix if before is None else join(prefix, before)
        total = running
        stride *= size
    return before[1]


def attention_kernel(first_ref, turn_ref, q_ref, own_ref, z1_ref, z2_ref, r1_ref, r2_ref, r3_ref,
                     out_ref, key_s, value_s, query_s, mixed_s, score_s):
    rows = own_ref.shape[0]
    local_kv = own_ref.shape[1] // (2 * HEAD_DIM)
    groups = HEADS // KV_HEADS
    tiles = WINDOW // rows + 1
    first = first_ref[0]
    turn = turn_ref[0]
    lane = lax.broadcasted_iota(jnp.int32, (rows, LANES - HEAD_DIM), 1)
    one = jnp.where(lane == 0, 1.0, 0.0).astype(BF16)
    moved = (None, r1_ref, r2_ref, r3_ref)
    for tile in range(tiles):
        if tile % 4 == 0:
            block = (z2_ref, z1_ref, own_ref)[tile // 4][...]
        else:
            step = 4 - tile % 4
            early = tile < 4
            part = jnp.where((turn < step) == early, 1, 0)
            block = moved[step][part]
        closed = jnp.where(tile < first, LOW, 0.0)
        extra = jnp.where(lane == 0, closed, 0.0).astype(BF16)
        for head in range(local_kv):
            key = block[:, head * HEAD_DIM : (head + 1) * HEAD_DIM]
            value = block[:, (local_kv + head) * HEAD_DIM : (local_kv + head + 1) * HEAD_DIM]
            key_s[head, tile * rows : (tile + 1) * rows, :] = jnp.concatenate((key, extra), axis=1)
            value_s[head, tile * rows : (tile + 1) * rows, :] = jnp.concatenate((value, one), axis=1)
    for head in range(local_kv * groups):
        query = q_ref[:, head * HEAD_DIM : (head + 1) * HEAD_DIM]
        query_s[head] = jnp.concatenate((query, one), axis=1)
    qpos = lax.broadcasted_iota(jnp.int32, (rows, rows), 0)
    cpos = lax.broadcasted_iota(jnp.int32, (rows, rows), 1)
    factor = HEAD_DIM ** (-0.5) * LOG2E

    for kv in range(local_kv):

        def one_head(index, carry):
            head = kv * groups + index
            query = query_s[head]
            top = jnp.full((rows, LANES), -jnp.inf, F32)
            for tile in range(tiles):
                key = key_s[kv, tile * rows : (tile + 1) * rows, :]
                score = lax.dot_general(query, key, (((1,), (1,)), ((), ())), preferred_element_type=F32)
                if tile == 0:
                    score = jnp.where(cpos > qpos, score, -jnp.inf)
                if tile == tiles - 1:
                    score = jnp.where(cpos <= qpos, score, -jnp.inf)
                score_s[:, tile * rows : (tile + 1) * rows] = score
                for piece in range(rows // LANES):
                    top = jnp.maximum(top, score[:, piece * LANES : (piece + 1) * LANES])
            best = jnp.max(top, axis=1, keepdims=True)
            total = jnp.zeros((rows, LANES), F32)
            mixed = jnp.zeros((rows, LANES), F32)
            for tile in range(tiles):
                prob = jnp.exp2((score_s[:, tile * rows : (tile + 1) * rows] - best) * factor)
                for piece in range(rows // LANES):
                    total = total + prob[:, piece * LANES : (piece + 1) * LANES]
                value = value_s[kv, tile * rows : (tile + 1) * rows, :]
                mixed = mixed + jnp.dot(prob.astype(BF16), value, preferred_element_type=F32)
            mixed_s[head] = (mixed / jnp.sum(total, axis=1, keepdims=True)).astype(BF16)
            return carry

        lax.fori_loop(0, groups, one_head, 0)
    for head in range(local_kv * groups):
        out_ref[:, head * HEAD_DIM : (head + 1) * HEAD_DIM] = mixed_s[head][:, :HEAD_DIM]


def attention_part(queries, keys, att_values):
    rows = queries.shape[0]
    count = lax.axis_size("seq")
    place = lax.axis_index("seq")
    turn = place % 4
    local_heads = queries.shape[1] // HEAD_DIM
    local_kv = keys.shape[1] // HEAD_DIM
    tiles = WINDOW // rows + 1
    own = jnp.concatenate((keys, att_values), axis=1)
    z1 = shifted(own, "seq", 4)
    z2 = shifted(own, "seq", 8)
    moved = []
    for step in (1, 2, 3):
        payload = jnp.stack((z1, jnp.where(turn + step >= 4, z2, own)))
        pairs = [(i, i - i % 4 + (i + step) % 4) for i in range(count)]
        moved.append(lax.ppermute(payload, "seq", pairs))
    first = jnp.maximum(tiles - 1 - place, 0).astype(jnp.int32).reshape(1)
    smem = pl.BlockSpec(memory_space=pltpu.SMEM)
    vmem = pl.BlockSpec(memory_space=pltpu.VMEM)
    pairs = rows * rows * tiles * local_heads
    return pl.pallas_call(
        attention_kernel,
        in_specs=[smem, smem] + [vmem] * 7,
        out_specs=vmem,
        out_shape=jax.ShapeDtypeStruct(queries.shape, BF16),
        scratch_shapes=[
            pltpu.VMEM((local_kv, tiles * rows, LANES), BF16),
            pltpu.VMEM((local_kv, tiles * rows, LANES), BF16),
            pltpu.VMEM((local_heads, rows, LANES), BF16),
            pltpu.VMEM((local_heads, rows, LANES), BF16),
            pltpu.VMEM((rows, tiles * rows), F32),
        ],
        compiler_params=params(48),
        cost_estimate=cost(pairs * 1200, rows * 4096 * 3, pairs),
        name="attention",
    )(first, turn.astype(jnp.int32).reshape(1), queries, own, z1, z2, *moved)


def local(
    mamba_in, mamba_gate, conv_weight, conv_bias, x_proj, dt_proj, dt_bias, a_log, d_skip,
    queries, keys, att_values, logits, targets, allowed,
):
    rows, channels = mamba_in.shape
    taps = conv_weight.shape[0]
    rank = dt_proj.shape[0]
    nstate = a_log.shape[0]
    subs = channels // LANES
    rim = shifted(mamba_in[rows - (taps - 1) :], "seq", 1)
    stats = scoring_part(logits, targets, allowed)
    conv_out, part = convolve(mamba_in, rim, conv_weight, conv_bias, x_proj)
    proj = part + swapped(part)
    dt_low = proj[:, :rank].astype(BF16)
    b_wide = jnp.broadcast_to(proj[:, rank : rank + nstate].reshape(rows * nstate, 1), (rows * nstate, LANES))
    c_wide = jnp.broadcast_to(proj[:, rank + nstate :].reshape(rows * nstate, 1), (rows * nstate, LANES))
    folded = a_log.reshape(nstate, subs, LANES)
    y, cum, end = local_scan(dt_low, dt_proj, dt_bias, folded, d_skip, conv_out, b_wide, c_wide)
    incoming = entering(cum[rows - 1], end, -jnp.exp(folded))
    attention_out = attention_part(queries, keys, att_values)
    loglik = scoring_join(stats, swapped(stats))
    mamba_out = finish(y, cum, c_wide, incoming, folded, mamba_gate)
    return (mamba_out, attention_out, loglik)


def solution(mesh):
    in_specs = (
        P("seq", "vocab"),
        P("seq", "vocab"),
        P(None, "vocab"),
        P("vocab"),
        P("vocab", None),
        P(None, "vocab"),
        P("vocab"),
        P(None, "vocab"),
        P("vocab"),
        P("seq", "vocab"),
        P("seq", "vocab"),
        P("seq", "vocab"),
        P("seq", "vocab"),
        P("seq"),
        P("seq", "vocab"),
    )
    out_specs = (P("seq", "vocab"), P("seq", "vocab"), P("seq"))
    return jax.shard_map(local, mesh=mesh, in_specs=in_specs, out_specs=out_specs, check_vma=False)
```

time: 730 us -> 150 us (0.21)
  the two profiles are of different devices: /device:TPU:254 before, /device:TPU:32 now
where the time goes in v1:
time: 150 us; the launch traced here: 148 us
  Pallas kernels  75.1 us (50%)
  starting transfers between devices  36.2 us (24%)
  waiting for transfers between devices  15.3 us (10%)
  local copies, waits for them, and re-layouts  14.5 us (10%)
  other arithmetic  5.49 us (4%)
    pallas_call x1, Pallas kernels, local_scan(): pl.pallas_call(scan_kernel, grid=(channels // GROUP,), in_specs=[pl.Block...  24.9 us
    pallas_call x1, Pallas kernels, attention_part(): pl.pallas_call(attention_kernel, in_specs=[smem, smem] + [vmem] * 7, out_...  22.5 us
    ppermute x10, starting transfers between devices, entering(): came.append(lax.ppermute(message, 'seq', pairs))  17 us
    pallas_call x1, Pallas kernels, finish(): pl.pallas_call(finish_kernel, grid=(channels // GROUP,), in_specs=[folded...  16.5 us
    ppermute x3, starting transfers between devices, shifted(): lax.ppermute(value, axis, [(source, source + steps) for source in range(l...  13.7 us
    unnamed x42, local copies, waits for them, and re-layouts  9.96 us
    ppermute x10, waiting for transfers between devices, entering(): came.append(lax.ppermute(message, 'seq', pairs))  9.24 us
    pallas_call x1, Pallas kernels, scoring_part(): pl.pallas_call(score_kernel, grid=(rows // block,), in_specs=[pl.BlockSpe...  6.68 us
  transfers between devices with their start and end apart: 18, of which 8 were waited for; matrix products, arithmetic and copies ran while one was open for 9% of the time, Pallas kernels for 40%

profile of v1, /device:TPU:32, one launch (start us, length us, event | category | flops | bytes accessed | tf_op | source)
XLA Modules:
  0.0 147.9 jit_solution(17694076235449027388)
XLA Ops:
  0.6 0.8 slice.153
  1.4 3.5 %collective-permute-start = (bf16[3,3072]{1,0:T(4,128)(2,1)S(1)}, bf16[3,3072]{1,0:T(4,128)(2,1)S(1)}, u32[]{:S(2)}, u32[]{:S(2)}) collective-permute-start(bf16[3,3072]{1,0:T(4,128)(2,1)S(1)} %slice.153), channel_id=1, source_target_pairs={{0,2},{2,4},{4,6},{6,8},{8,10},{10,12},{12,14},{14,16},{16,18},{18... | collective-permute-start | bytes 55304 | tf_op jit(solution)/shard_map/ppermute | solution.py:31
  4.9 0.7 broadcast_subtract_fusion
  5.8 2.2 %copy-done = bf16[256,8192]{1,0:T(8,128)(2,1)S(1)} copy-done((bf16[256,8192]{1,0:T(8,128)(2,1)S(1)}, bf16[256,8192]{1,0:T(8,128)(2,1)}, u32[]{:S(2)}) %copy-start) | copy-done | bytes 4194328
  8.0 1.2 copy-done.3
  9.2 6.7 %scoring.1 = f32[256,128]{1,0:T(8,128)S(1)} custom-call(bf16[256,8192]{1,0:T(8,128)(2,1)S(1)} %copy-done, s32[256,1024]{1,0:T(8,128)S(1)} %copy-done.3, s32[256,1]{1,0:T(8,128)S(1)} %copy.24.local_target_ref), custom_call_target="tpu_custom_call" | custom-call | flops 536870912 | bytes 6291456 | tf_op jit(solution)/shard_map/scoring/pallas_call | solution.py:78
  15.9 0.7 slice_bitcast_fusion
  16.7 1.8 %copy.21.proj_ref = bf16[3072,224]{1,0:T(8,128)(2,1)S(1)} copy(bf16[3072,224]{0,1:T(8,128)(2,1)} %param.19) | data formatting | bytes 2752512 | tf_op args[4]
  18.5 0.8 copy.23
  19.2 0.8 copy.22
  20.0 4.6 %convolution.1 = (bf16[256,3072]{1,0:T(8,128)(2,1)S(1)}, f32[256,224]{1,0:T(8,128)S(1)}) custom-call(bf16[256,3072]{1,0:T(8,128)(2,1)S(1)} %copy-done.2, bf16[3,3072]{1,0:T(4,128)(2,1)S(1)} %collective-permute-done.rim_ref, f32[4,3072]{1,0:T(4,128)S(1)} %copy-done.4, f32[1,3072]{1,0:T(1,128)S(1)} %bitcast.47, bf16[3072,224]{1,0:T(8,128)(2,1)S(1)} %copy.21.proj_ref), custom_call_target="tpu_custom_call" | custom-call | flops 550502400 | bytes 3145728 | tf_op jit(solution)/shard_map/convolution/pallas_call | solution.py:129
  24.6 1.1 copy-done.7
  25.7 0.4 collective-permute-start.1
  26.3 3.8 %collective-permute-start.12 = (bf16[256,384]{1,0:T(8,128)(2,1)S(1)}, bf16[256,384]{1,0:T(8,128)(2,1)S(1)}, u32[]{:S(2)}, u32[]{:S(2)}) collective-permute-start(bf16[256,384]{1,0:T(8,128)(2,1)S(1)} %pad_maximum_fusion.3.own_ref), channel_id=1, source_target_pairs={{0,8},{2,10},{4,12},{6,14},{8,16},{10,18},{12,20},{14,22},{16,24},... | collective-permute-start | bytes 589832 | tf_op jit(solution)/shard_map/ppermute | solution.py:31
  30.1 6.4 %collective-permute-start.13 = (bf16[256,384]{1,0:T(8,128)(2,1)S(1)}, bf16[256,384]{1,0:T(8,128)(2,1)S(1)}, u32[]{:S(2)}, u32[]{:S(2)}) collective-permute-start(bf16[256,384]{1,0:T(8,128)(2,1)S(1)} %pad_maximum_fusion.3.own_ref), channel_id=1, source_target_pairs={{0,16},{2,18},{4,20},{6,22},{8,24},{10,26},{12,28},{14,30},{16,32}... | collective-permute-start | bytes 589832 | tf_op jit(solution)/shard_map/ppermute | solution.py:31
  36.7 1.0 copy.25
  37.7 1.6 %fusion.8 = (f32[256]{0:T(256)S(1)}, f32[256]{0:T(256)S(1)}, f32[256]{0:T(256)S(1)}, f32[256]{0:T(256)S(1)}, f32[256]{0:T(256)S(1)}) fusion(f32[8,256]{0,1:T(8,128)} %collective-permute-done.17, f32[8,256]{0,1:T(8,128)} %slice_bitcast_fusion), kind=kLoop, calls=%fused_computation.32 | loop fusion | flops 256 | bytes 11264 | tf_op jit(solution)/shard_map/add | solution.py:98
  39.7 0.6 broadcast_in_dim.9.b_ref
  40.4 2.0 %broadcast_in_dim.11.c_ref = f32[4096,128]{1,0:T(8,128)} broadcast(f32[4096]{0:T(1024)S(1)} %broadcast_in_dim.10), dimensions={0} | broadcast | bytes 2113536 | tf_op jit(solution)/shard_map/broadcast_in_dim | solution.py:445
  42.4 24.9 %local_scan.1 = (f32[256,24,128]{2,1,0:T(8,128)}, f32[256,24,128]{2,1,0:T(8,128)}, f32[16,24,128]{2,1,0:T(8,128)S(1)}) custom-call(bf16[256,192]{1,0:T(8,128)(2,1)S(1)} %slice.450.low_ref, bf16[192,3072]{1,0:T(8,128)(2,1)S(1)} %copy-done.9, f32[1,3072]{1,0:T(1,128)S(1)} %bitcast.48, f32[16,24,128]{2,1,0:T(8,128)S(1)} %bitcast.44, f32[24,128]{1,0:T(8,128)S(1)} %bitcast.49, ...), custom_call_target="tpu_custom_call" | custom-call | flops 6291456000 | bytes 9437184 | tf_op jit(solution)/shard_map/local_scan/pallas_call | solution.py:205
  67.3 0.8 subtract_convert_fusion.3
  68.1 2.2 %collective-permute-start.2 = (bf16[18,24,128]{2,1,0:T(8,128)(2,1)S(1)}, bf16[18,24,128]{2,1,0:T(8,128)(2,1)S(1)}, u32[]{:S(2)}, u32[]{:S(2)}) collective-permute-start(bf16[18,24,128]{2,1,0:T(8,128)(2,1)S(1)} %pad_maximum_fusion.4), channel_id=1, source_target_pairs={{0,6},{2,4},{4,2},{6,0},{8,14},{10,12},{12,10},{14,8},{16,22},{18,... | collective-permute-start | bytes 331784 | tf_op jit(solution)/shard_map/ppermute | solution.py:306
  70.3 1.5 %collective-permute-start.3 = (bf16[18,24,128]{2,1,0:T(8,128)(2,1)S(1)}, bf16[18,24,128]{2,1,0:T(8,128)(2,1)S(1)}, u32[]{:S(2)}, u32[]{:S(2)}) collective-permute-start(bf16[18,24,128]{2,1,0:T(8,128)(2,1)S(1)} %pad_maximum_fusion.4), channel_id=1, source_target_pairs={{0,4},{2,6},{4,0},{6,2},{8,12},{10,14},{12,8},{14,10},{16,20},{18,... | collective-permute-start | bytes 331784 | tf_op jit(solution)/shard_map/ppermute | solution.py:306
  71.8 0.4 collective-permute-start.4
  72.3 0.6 log_subtract_fusion
  72.9 2.5 %collective-permute-done.2 = bf16[18,24,128]{2,1,0:T(8,128)(2,1)S(1)} collective-permute-done((bf16[18,24,128]{2,1,0:T(8,128)(2,1)S(1)}, bf16[18,24,128]{2,1,0:T(8,128)(2,1)S(1)}, u32[]{:S(2)}, u32[]{:S(2)}) %collective-permute-start.2) | collective-permute-done | bytes 110624 | tf_op jit(solution)/shard_map/ppermute | solution.py:306
  75.3 1.9 %collective-permute-done.3 = bf16[18,24,128]{2,1,0:T(8,128)(2,1)S(1)} collective-permute-done((bf16[18,24,128]{2,1,0:T(8,128)(2,1)S(1)}, bf16[18,24,128]{2,1,0:T(8,128)(2,1)S(1)}, u32[]{:S(2)}, u32[]{:S(2)}) %collective-permute-start.3) | collective-permute-done | bytes 110624 | tf_op jit(solution)/shard_map/ppermute | solution.py:306
  77.6 1.1 collective-permute-start.5
  78.7 0.2 select_bitcast_fusion
  78.9 3.6 %collective-permute-done.5 = bf16[18,24,128]{2,1,0:T(8,128)(2,1)S(1)} collective-permute-done((bf16[18,24,128]{2,1,0:T(8,128)(2,1)S(1)}, bf16[18,24,128]{2,1,0:T(8,128)(2,1)S(1)}, u32[]{:S(2)}, u32[]{:S(2)}) %collective-permute-start.5) | collective-permute-done | bytes 110624 | tf_op jit(solution)/shard_map/ppermute | solution.py:306
  82.7 1.5 %collective-permute-start.6 = (bf16[18,24,128]{2,1,0:T(8,128)(2,1)S(1)}, bf16[18,24,128]{2,1,0:T(8,128)(2,1)S(1)}, u32[]{:S(2)}, u32[]{:S(2)}) collective-permute-start(bf16[18,24,128]{2,1,0:T(8,128)(2,1)S(1)} %pad_maximum_fusion.6), channel_id=1, source_target_pairs={{0,48},{2,50},{4,52},{6,54},{8,56},{10,58},{12,60},{14,62},{16,32}... | collective-permute-start | bytes 331784 | tf_op jit(solution)/shard_map/ppermute | solution.py:306
  84.2 3.6 %collective-permute-start.7 = (bf16[18,24,128]{2,1,0:T(8,128)(2,1)S(1)}, bf16[18,24,128]{2,1,0:T(8,128)(2,1)S(1)}, u32[]{:S(2)}, u32[]{:S(2)}) collective-permute-start(bf16[18,24,128]{2,1,0:T(8,128)(2,1)S(1)} %pad_maximum_fusion.6), channel_id=1, source_target_pairs={{0,32},{2,34},{4,36},{6,38},{8,40},{10,42},{12,44},{14,46},{16,48}... | collective-permute-start | bytes 331784 | tf_op jit(solution)/shard_map/ppermute | solution.py:306
  87.8 1.4 collective-permute-start.8
  89.4 1.5 collective-permute-start.14
  90.8 2.0 %collective-permute-start.15 = (bf16[2,256,384]{2,1,0:T(8,128)(2,1)S(1)}, bf16[2,256,384]{2,1,0:T(8,128)(2,1)S(1)}, u32[]{:S(2)}, u32[]{:S(2)}) collective-permute-start(bf16[2,256,384]{2,1,0:T(8,128)(2,1)S(1)} %get-tuple-element.52), channel_id=1, source_target_pairs={{0,4},{2,6},{4,0},{6,2},{8,12},{10,14},{12,8},{14,10},{16,20},{18,... | collective-permute-start | bytes 1179656 | tf_op jit(solution)/shard_map/ppermute | solution.py:407
  92.8 0.4 collective-permute-done.6
  93.2 1.6 %collective-permute-start.16 = (bf16[2,256,384]{2,1,0:T(8,128)(2,1)S(1)}, bf16[2,256,384]{2,1,0:T(8,128)(2,1)S(1)}, u32[]{:S(2)}, u32[]{:S(2)}) collective-permute-start(bf16[2,256,384]{2,1,0:T(8,128)(2,1)S(1)} %get-tuple-element.51), channel_id=1, source_target_pairs={{0,6},{2,0},{4,2},{6,4},{8,14},{10,8},{12,10},{14,12},{16,22},{18,... | collective-permute-start | bytes 1179656 | tf_op jit(solution)/shard_map/ppermute | solution.py:407
  94.8 0.9 collective-permute-done.8
  96.0 2.9 %collective-permute-start.9 = (bf16[18,24,128]{2,1,0:T(8,128)(2,1)S(1)}, bf16[18,24,128]{2,1,0:T(8,128)(2,1)S(1)}, u32[]{:S(2)}, u32[]{:S(2)}) collective-permute-start(bf16[18,24,128]{2,1,0:T(8,128)(2,1)S(1)} %pad_maximum_fusion.7), channel_id=1, source_target_pairs={{0,192},{2,194},{4,196},{6,198},{8,200},{10,202},{12,204},{14,206}... | collective-permute-start | bytes 331784 | tf_op jit(solution)/shard_map/ppermute | solution.py:306
  98.9 0.8 collective-permute-start.10
  99.6 2.8 %collective-permute-done.14.r1_ref = bf16[2,256,384]{2,1,0:T(8,128)(2,1)S(1)} collective-permute-done((bf16[2,256,384]{2,1,0:T(8,128)(2,1)S(1)}, bf16[2,256,384]{2,1,0:T(8,128)(2,1)S(1)}, u32[]{:S(2)}, u32[]{:S(2)}) %collective-permute-start.14) | collective-permute-done | bytes 393248 | tf_op jit(solution)/shard_map/ppermute | solution.py:407
  102.4 1.5 %collective-permute-start.11 = (bf16[18,24,128]{2,1,0:T(8,128)(2,1)S(1)}, bf16[18,24,128]{2,1,0:T(8,128)(2,1)S(1)}, u32[]{:S(2)}, u32[]{:S(2)}) collective-permute-start(bf16[18,24,128]{2,1,0:T(8,128)(2,1)S(1)} %pad_maximum_fusion.7), channel_id=1, source_target_pairs={{0,64},{2,66},{4,68},{6,70},{8,72},{10,74},{12,76},{14,78},{16,80}... | collective-permute-start | bytes 331784 | tf_op jit(solution)/shard_map/ppermute | solution.py:306
  104.0 2.7 %collective-permute-done.15.r2_ref = bf16[2,256,384]{2,1,0:T(8,128)(2,1)S(1)} collective-permute-done((bf16[2,256,384]{2,1,0:T(8,128)(2,1)S(1)}, bf16[2,256,384]{2,1,0:T(8,128)(2,1)S(1)}, u32[]{:S(2)}, u32[]{:S(2)}) %collective-permute-start.15) | collective-permute-done | bytes 393248 | tf_op jit(solution)/shard_map/ppermute | solution.py:407
  106.7 0.6 collective-permute-done.16.r3_ref
  107.2 22.5 %attention.1 = bf16[256,1536]{1,0:T(8,128)(2,1)} custom-call(s32[1]{0:T(128)} %bitcast.15.first_ref, s32[1]{0:T(128)} %bitcast.16.turn_ref, bf16[256,1536]{1,0:T(8,128)(2,1)S(1)} %copy-done.10, bf16[256,384]{1,0:T(8,128)(2,1)S(1)} %pad_maximum_fusion.3.own_ref, bf16[256,384]{1,0:T(8,128)(2,1)S(1)} %collective-permute-done.12.z1_ref, ...), custom_call_target="tpu_custom_call" | custom-call | flops 11324620800 | bytes 3145728 | tf_op jit(solution)/shard_map/attention/pallas_call | solution.py:412
  129.9 0.5 fusion.4.state_ref
  130.4 1.1 copy-done.1
  131.4 16.5 %finish.1 = bf16[256,3072]{1,0:T(8,128)(2,1)} custom-call(f32[256,24,128]{2,1,0:T(8,128)} %get-tuple-element.10.y_ref, f32[256,24,128]{2,1,0:T(8,128)} %get-tuple-element.11.cum_ref, f32[4096,128]{1,0:T(8,128)S(1)} %copy-done.1, f32[16,24,128]{2,1,0:T(8,128)S(1)} %fusion.4.state_ref, f32[16,24,128]{2,1,0:T(8,128)S(1)} %bitcast.45, ...), custom_call_target="tpu_custom_call" | custom-call | flops 3774873600 | bytes 9437184 | tf_op jit(solution)/shard_map/finish/pallas_call | solution.py:260
  (77 shorter events, 1.9 us)
Async XLA Ops:
  1.4 18.6 %collective-permute-start = (bf16[3,3072]{1,0:T(4,128)(2,1)S(1)}, bf16[3,3072]{1,0:T(4,128)(2,1)S(1)}, u32[]{:S(2)}, u32[]{:S(2)}) collective-permute-start(bf16[3,3072]{1,0:T(4,128)(2,1)S(1)} %slice.153), channel_id=1, source_target_pairs={{0,2},{2,4},{4,6},{6,8},{8,10},{10,12},{12,14},{14,16},{16,18},{18... | collective-permute-start | bytes 55304 | tf_op jit(solution)/shard_map/ppermute | solution.py:31
  5.8 2.2 %copy-start = (bf16[256,8192]{1,0:T(8,128)(2,1)S(1)}, bf16[256,8192]{1,0:T(8,128)(2,1)}, u32[]{:S(2)}) copy-start(bf16[256,8192]{1,0:T(8,128)(2,1)} %logits_ref.1) | copy-start | bytes 12582916
  8.0 1.2 copy-start.3
  15.9 2.6 %copy-start.17 = (bf16[256,192]{0,1:T(8,128)(2,1)S(1)}, bf16[256,192]{0,1:T(8,128)(2,1)}, u32[]{:S(2)}) copy-start(bf16[256,192]{0,1:T(8,128)(2,1)} %param.26) | copy-start | bytes 294916
  16.6 2.7 %copy-start.18 = (bf16[256,192]{0,1:T(8,128)(2,1)S(1)}, bf16[256,192]{0,1:T(8,128)(2,1)}, u32[]{:S(2)}) copy-start(bf16[256,192]{0,1:T(8,128)(2,1)} %param.25) | copy-start | bytes 294916
  16.6 3.4 %copy-start.2 = (bf16[256,3072]{1,0:T(8,128)(2,1)S(1)}, bf16[256,3072]{1,0:T(8,128)(2,1)}, u32[]{:S(2)}) copy-start(bf16[256,3072]{1,0:T(8,128)(2,1)} %x_ref.1) | copy-start | bytes 4718596
  16.6 3.4 %copy-start.4 = (f32[4,3072]{1,0:T(4,128)S(1)}, f32[4,3072]{1,0:T(4,128)}, u32[]{:S(2)}) copy-start(f32[4,3072]{1,0:T(4,128)} %weight_ref.1) | copy-start | bytes 147460
  16.6 3.4 %copy-start.5 = (f32[3072]{0:T(1024)S(1)}, f32[3072]{0:T(1024)}, u32[]{:S(2)}) copy-start(f32[3072]{0:T(1024)} %param.18) | copy-start | bytes 36868
  16.6 21.1 %collective-permute-start.17 = (f32[8,256]{0,1:T(8,128)}, f32[8,256]{0,1:T(8,128)}, u32[]{:S(2)}, u32[]{:S(2)}) collective-permute-start(f32[8,256]{0,1:T(8,128)} %slice_bitcast_fusion), channel_id=1, source_target_pairs={{0,1},{1,0},{2,3},{3,2},{4,5},{5,4},{6,7},{7,6},{8,9},{9,8},{10,11... | collective-permute-start | bytes 24584 | tf_op jit(solution)/shard_map/ppermute | solution.py:35
  20.0 6.1 %copy-start.13 = (bf16[256,192]{1,0:T(8,128)(2,1)S(1)}, bf16[256,192]{1,0:T(8,128)(2,1)}, u32[]{:S(2)}) copy-start(bf16[256,192]{1,0:T(8,128)(2,1)} %copy.23) | copy-start | bytes 294916
  20.0 6.1 %copy-start.15 = (bf16[256,192]{1,0:T(8,128)(2,1)S(1)}, bf16[256,192]{1,0:T(8,128)(2,1)}, u32[]{:S(2)}) copy-start(bf16[256,192]{1,0:T(8,128)(2,1)} %copy.22) | copy-start | bytes 294916
  24.6 1.1 copy-start.7
  25.7 13.5 %collective-permute-start.1 = (f32[256,224]{1,0:T(8,128)S(1)}, f32[256,224]{1,0:T(8,128)S(1)}, u32[]{:S(2)}, u32[]{:S(2)}) collective-permute-start(f32[256,224]{1,0:T(8,128)S(1)} %get-tuple-element.8), channel_id=1, source_target_pairs={{0,1},{1,0},{2,3},{3,2},{4,5},{5,4},{6,7},{7,6},{8,9},{9,8},{10,11... | collective-permute-start | bytes 688136 | tf_op jit(solution)/shard_map/ppermute | solution.py:35
  26.3 63.0 %collective-permute-start.12 = (bf16[256,384]{1,0:T(8,128)(2,1)S(1)}, bf16[256,384]{1,0:T(8,128)(2,1)S(1)}, u32[]{:S(2)}, u32[]{:S(2)}) collective-permute-start(bf16[256,384]{1,0:T(8,128)(2,1)S(1)} %pad_maximum_fusion.3.own_ref), channel_id=1, source_target_pairs={{0,8},{2,10},{4,12},{6,14},{8,16},{10,18},{12,20},{14,22},{16,24},... | collective-permute-start | bytes 589832 | tf_op jit(solution)/shard_map/ppermute | solution.py:31
  30.1 48.6 %collective-permute-start.13 = (bf16[256,384]{1,0:T(8,128)(2,1)S(1)}, bf16[256,384]{1,0:T(8,128)(2,1)S(1)}, u32[]{:S(2)}, u32[]{:S(2)}) collective-permute-start(bf16[256,384]{1,0:T(8,128)(2,1)S(1)} %pad_maximum_fusion.3.own_ref), channel_id=1, source_target_pairs={{0,16},{2,18},{4,20},{6,22},{8,24},{10,26},{12,28},{14,30},{16,32}... | collective-permute-start | bytes 589832 | tf_op jit(solution)/shard_map/ppermute | solution.py:31
  39.7 2.7 %copy-start.9 = (bf16[192,3072]{1,0:T(8,128)(2,1)S(1)}, bf16[192,3072]{1,0:T(8,128)(2,1)}, u32[]{:S(2)}) copy-start(bf16[192,3072]{1,0:T(8,128)(2,1)} %dt_ref.1) | copy-start | bytes 3538948
  40.3 2.0 %copy-start.8 = (bf16[256,3072]{1,0:T(8,128)(2,1)S(1)}, bf16[256,3072]{1,0:T(8,128)(2,1)}, u32[]{:S(2)}) copy-start(bf16[256,3072]{1,0:T(8,128)(2,1)} %copy-done.7) | copy-start | bytes 4718596
  40.3 2.0 %copy-start.11 = (f32[3072]{0:T(1024)S(1)}, f32[3072]{0:T(1024)}, u32[]{:S(2)}) copy-start(f32[3072]{0:T(1024)} %param.21) | copy-start | bytes 36868
  40.3 2.0 %copy-start.12 = (f32[3072]{0:T(1024)S(1)}, f32[3072]{0:T(1024)}, u32[]{:S(2)}) copy-start(f32[3072]{0:T(1024)} %param.23) | copy-start | bytes 36868
  68.1 7.2 %collective-permute-start.2 = (bf16[18,24,128]{2,1,0:T(8,128)(2,1)S(1)}, bf16[18,24,128]{2,1,0:T(8,128)(2,1)S(1)}, u32[]{:S(2)}, u32[]{:S(2)}) collective-permute-start(bf16[18,24,128]{2,1,0:T(8,128)(2,1)S(1)} %pad_maximum_fusion.4), channel_id=1, source_target_pairs={{0,6},{2,4},{4,2},{6,0},{8,14},{10,12},{12,10},{14,8},{16,22},{18,... | collective-permute-start | bytes 331784 | tf_op jit(solution)/shard_map/ppermute | solution.py:306
  70.3 7.0 %collective-permute-start.3 = (bf16[18,24,128]{2,1,0:T(8,128)(2,1)S(1)}, bf16[18,24,128]{2,1,0:T(8,128)(2,1)S(1)}, u32[]{:S(2)}, u32[]{:S(2)}) collective-permute-start(bf16[18,24,128]{2,1,0:T(8,128)(2,1)S(1)} %pad_maximum_fusion.4), channel_id=1, source_target_pairs={{0,4},{2,6},{4,0},{6,2},{8,12},{10,14},{12,8},{14,10},{16,20},{18,... | collective-permute-start | bytes 331784 | tf_op jit(solution)/shard_map/ppermute | solution.py:306
  71.8 5.4 %collective-permute-start.4 = (bf16[18,24,128]{2,1,0:T(8,128)(2,1)S(1)}, bf16[18,24,128]{2,1,0:T(8,128)(2,1)S(1)}, u32[]{:S(2)}, u32[]{:S(2)}) collective-permute-start(bf16[18,24,128]{2,1,0:T(8,128)(2,1)S(1)} %pad_maximum_fusion.4), channel_id=1, source_target_pairs={{0,2},{2,0},{4,6},{6,4},{8,10},{10,8},{12,14},{14,12},{16,18},{18,... | collective-permute-start | bytes 331784 | tf_op jit(solution)/shard_map/ppermute | solution.py:306
  72.9 5.8 %copy-start.14 = (bf16[256,192]{1,0:T(8,128)(2,1)S(1)}, bf16[256,192]{1,0:T(8,128)(2,1)}, u32[]{:S(2)}) copy-start(bf16[256,192]{1,0:T(8,128)(2,1)} %copy.23) | copy-start | bytes 294916
  72.9 5.8 %copy-start.16 = (bf16[256,192]{1,0:T(8,128)(2,1)S(1)}, bf16[256,192]{1,0:T(8,128)(2,1)}, u32[]{:S(2)}) copy-start(bf16[256,192]{1,0:T(8,128)(2,1)} %copy.22) | copy-start | bytes 294916
  77.6 4.8 %collective-permute-start.5 = (bf16[18,24,128]{2,1,0:T(8,128)(2,1)S(1)}, bf16[18,24,128]{2,1,0:T(8,128)(2,1)S(1)}, u32[]{:S(2)}, u32[]{:S(2)}) collective-permute-start(bf16[18,24,128]{2,1,0:T(8,128)(2,1)S(1)} %pad_maximum_fusion.5), channel_id=1, source_target_pairs={{0,8},{2,10},{4,12},{6,14},{8,0},{10,2},{12,4},{14,6},{16,24},{18,... | collective-permute-start | bytes 331784 | tf_op jit(solution)/shard_map/ppermute | solution.py:306
  82.7 10.5 %collective-permute-start.6 = (bf16[18,24,128]{2,1,0:T(8,128)(2,1)S(1)}, bf16[18,24,128]{2,1,0:T(8,128)(2,1)S(1)}, u32[]{:S(2)}, u32[]{:S(2)}) collective-permute-start(bf16[18,24,128]{2,1,0:T(8,128)(2,1)S(1)} %pad_maximum_fusion.6), channel_id=1, source_target_pairs={{0,48},{2,50},{4,52},{6,54},{8,56},{10,58},{12,60},{14,62},{16,32}... | collective-permute-start | bytes 331784 | tf_op jit(solution)/shard_map/ppermute | solution.py:306
  84.2 10.6 %collective-permute-start.7 = (bf16[18,24,128]{2,1,0:T(8,128)(2,1)S(1)}, bf16[18,24,128]{2,1,0:T(8,128)(2,1)S(1)}, u32[]{:S(2)}, u32[]{:S(2)}) collective-permute-start(bf16[18,24,128]{2,1,0:T(8,128)(2,1)S(1)} %pad_maximum_fusion.6), channel_id=1, source_target_pairs={{0,32},{2,34},{4,36},{6,38},{8,40},{10,42},{12,44},{14,46},{16,48}... | collective-permute-start | bytes 331784 | tf_op jit(solution)/shard_map/ppermute | solution.py:306
  87.8 7.8 %collective-permute-start.8 = (bf16[18,24,128]{2,1,0:T(8,128)(2,1)S(1)}, bf16[18,24,128]{2,1,0:T(8,128)(2,1)S(1)}, u32[]{:S(2)}, u32[]{:S(2)}) collective-permute-start(bf16[18,24,128]{2,1,0:T(8,128)(2,1)S(1)} %pad_maximum_fusion.6), channel_id=1, source_target_pairs={{0,16},{2,18},{4,20},{6,22},{8,24},{10,26},{12,28},{14,30},{16,0},... | collective-permute-start | bytes 331784 | tf_op jit(solution)/shard_map/ppermute | solution.py:306
  89.4 13.1 %collective-permute-start.14 = (bf16[2,256,384]{2,1,0:T(8,128)(2,1)S(1)}, bf16[2,256,384]{2,1,0:T(8,128)(2,1)S(1)}, u32[]{:S(2)}, u32[]{:S(2)}) collective-permute-start(bf16[2,256,384]{2,1,0:T(8,128)(2,1)S(1)} %get-tuple-element.53), channel_id=1, source_target_pairs={{0,2},{2,4},{4,6},{6,0},{8,10},{10,12},{12,14},{14,8},{16,18},{18,... | collective-permute-start | bytes 1179656 | tf_op jit(solution)/shard_map/ppermute | solution.py:407
  90.8 15.8 %collective-permute-start.15 = (bf16[2,256,384]{2,1,0:T(8,128)(2,1)S(1)}, bf16[2,256,384]{2,1,0:T(8,128)(2,1)S(1)}, u32[]{:S(2)}, u32[]{:S(2)}) collective-permute-start(bf16[2,256,384]{2,1,0:T(8,128)(2,1)S(1)} %get-tuple-element.52), channel_id=1, source_target_pairs={{0,4},{2,6},{4,0},{6,2},{8,12},{10,14},{12,8},{14,10},{16,20},{18,... | collective-permute-start | bytes 1179656 | tf_op jit(solution)/shard_map/ppermute | solution.py:407
  93.2 14.0 %copy-start.10 = (bf16[256,1536]{1,0:T(8,128)(2,1)S(1)}, bf16[256,1536]{1,0:T(8,128)(2,1)}, u32[]{:S(2)}) copy-start(bf16[256,1536]{1,0:T(8,128)(2,1)} %q_ref.1) | copy-start | bytes 2359300
  93.2 14.0 %collective-permute-start.16 = (bf16[2,256,384]{2,1,0:T(8,128)(2,1)S(1)}, bf16[2,256,384]{2,1,0:T(8,128)(2,1)S(1)}, u32[]{:S(2)}, u32[]{:S(2)}) collective-permute-start(bf16[2,256,384]{2,1,0:T(8,128)(2,1)S(1)} %get-tuple-element.51), channel_id=1, source_target_pairs={{0,6},{2,0},{4,2},{6,4},{8,14},{10,8},{12,10},{14,12},{16,22},{18,... | collective-permute-start | bytes 1179656 | tf_op jit(solution)/shard_map/ppermute | solution.py:407
  96.0 33.8 %collective-permute-start.9 = (bf16[18,24,128]{2,1,0:T(8,128)(2,1)S(1)}, bf16[18,24,128]{2,1,0:T(8,128)(2,1)S(1)}, u32[]{:S(2)}, u32[]{:S(2)}) collective-permute-start(bf16[18,24,128]{2,1,0:T(8,128)(2,1)S(1)} %pad_maximum_fusion.7), channel_id=1, source_target_pairs={{0,192},{2,194},{4,196},{6,198},{8,200},{10,202},{12,204},{14,206}... | collective-permute-start | bytes 331784 | tf_op jit(solution)/shard_map/ppermute | solution.py:306
  98.9 30.9 %collective-permute-start.10 = (bf16[18,24,128]{2,1,0:T(8,128)(2,1)S(1)}, bf16[18,24,128]{2,1,0:T(8,128)(2,1)S(1)}, u32[]{:S(2)}, u32[]{:S(2)}) collective-permute-start(bf16[18,24,128]{2,1,0:T(8,128)(2,1)S(1)} %pad_maximum_fusion.7), channel_id=1, source_target_pairs={{0,128},{2,130},{4,132},{6,134},{8,136},{10,138},{12,140},{14,142}... | collective-permute-start | bytes 331784 | tf_op jit(solution)/shard_map/ppermute | solution.py:306
  102.4 27.3 %collective-permute-start.11 = (bf16[18,24,128]{2,1,0:T(8,128)(2,1)S(1)}, bf16[18,24,128]{2,1,0:T(8,128)(2,1)S(1)}, u32[]{:S(2)}, u32[]{:S(2)}) collective-permute-start(bf16[18,24,128]{2,1,0:T(8,128)(2,1)S(1)} %pad_maximum_fusion.7), channel_id=1, source_target_pairs={{0,64},{2,66},{4,68},{6,70},{8,72},{10,74},{12,76},{14,78},{16,80}... | collective-permute-start | bytes 331784 | tf_op jit(solution)/shard_map/ppermute | solution.py:306
  107.2 23.1 %copy-start.6 = (bf16[256,3072]{1,0:T(8,128)(2,1)S(1)}, bf16[256,3072]{1,0:T(8,128)(2,1)}, u32[]{:S(2)}) copy-start(bf16[256,3072]{1,0:T(8,128)(2,1)} %gate_ref.1) | copy-start | bytes 4718596
  129.8 1.6 %copy-start.1 = (f32[4096,128]{1,0:T(8,128)S(1)}, f32[4096,128]{1,0:T(8,128)}, u32[]{:S(2)}) copy-start(f32[4096,128]{1,0:T(8,128)} %broadcast_in_dim.11.c_ref) | copy-start | bytes 6291460

commit v2 on v1

v2 whole, which is shorter than its diff:
```python
import functools

import jax
import jax.numpy as jnp
from jax import lax
from jax.experimental import pallas as pl
from jax.experimental.pallas import tpu as pltpu
from jax.sharding import PartitionSpec as P

HEADS = 32
KV_HEADS = 4
HEAD_DIM = 96
WINDOW = 2048
LOG2E = 1.4426950408889634
F32 = jnp.float32
BF16 = jnp.bfloat16
GROUP = 1024
LANES = 128
LOW = -1e30
PIECES = 4
TOKENS = 16


def params(mib):
    return pltpu.CompilerParams(vmem_limit_bytes=mib * 1024 * 1024)


def cost(flops, nbytes, trans=0):
    return pl.CostEstimate(flops=int(flops), bytes_accessed=int(nbytes), transcendentals=int(trans))


def shifted(value, axis, steps):
    count = lax.axis_size(axis)
    leading, last = (max(0, -steps), min(count, count - steps))
    return lax.ppermute(value, axis, [(source, source + steps) for source in range(leading, last)])


def swapped(value):
    return lax.ppermute(value, "vocab", [(0, 1), (1, 0)])


def score_kernel(logits_ref, allowed_ref, local_target_ref, *refs):
    out_ref = refs[-1]
    rows, width = logits_ref.shape
    words = LANES
    span = words * 8
    row_id = lax.broadcasted_iota(jnp.int32, (words, span), 0)
    col_id = lax.broadcasted_iota(jnp.int32, (words, span), 1)
    expand = jnp.where(row_id == col_id // 8, 1.0, 0.0).astype(BF16)
    col = lax.broadcasted_iota(jnp.int32, (rows, span), 1)
    bit = jnp.left_shift(jnp.int32(1), col & 7)
    wanted = local_target_ref[...]
    top = jnp.full((rows, LANES), -jnp.inf, F32)
    target = jnp.zeros((rows, LANES), F32)
    parts = []
    for block in range(width // span):
        values = logits_ref[:, block * span : (block + 1) * span].astype(F32)
        word = allowed_ref[:, block * words : (block + 1) * words].astype(F32).astype(BF16)
        spread = jnp.dot(word, expand, preferred_element_type=F32).astype(jnp.int32)
        masked = jnp.where((spread & bit) != 0, values, -jnp.inf)
        hit = jnp.where(col == wanted - block * span, values, 0.0)
        for piece in range(8):
            at = slice(piece * LANES, (piece + 1) * LANES)
            top = jnp.maximum(top, masked[:, at])
            target = target + hit[:, at]
        parts.append(masked)
    best = jnp.maximum(jnp.max(top, axis=1, keepdims=True), LOW)
    total = jnp.zeros((rows, LANES), F32)
    for masked in parts:
        terms = jnp.exp(masked - best)
        for piece in range(8):
            total = total + terms[:, piece * LANES : (piece + 1) * LANES]
    summed = jnp.sum(total, axis=1, keepdims=True)
    found = jnp.sum(target, axis=1, keepdims=True)
    lane = lax.broadcasted_iota(jnp.int32, (rows, LANES), 1)
    out_ref[...] = jnp.where(lane == 0, best, jnp.where(lane == 1, summed, found))


def scoring_part(logits, targets, allowed, after):
    rows, width = logits.shape
    block = 32
    local_target = (targets - lax.axis_index("vocab") * width).reshape(rows, 1)
    stats = pl.pallas_call(
        score_kernel,
        grid=(rows // block,),
        in_specs=[
            pl.BlockSpec((block, width), lambda i: (i, 0)),
            pl.BlockSpec((block, width // 8), lambda i: (i, 0)),
            pl.BlockSpec((block, 1), lambda i: (i, 0)),
        ]
        + [pl.BlockSpec(memory_space=pl.ANY)] * len(after),
        out_specs=pl.BlockSpec((block, LANES), lambda i: (i, 0)),
        out_shape=jax.ShapeDtypeStruct((rows, LANES), F32),
        compiler_params=params(48),
        cost_estimate=cost(rows * width * 256, rows * width * 3, rows * width),
        name="scoring",
    )(logits, allowed, local_target, *after)
    return stats[:, :8].T


def scoring_join(mine, other):
    top = jnp.maximum(mine[0], other[0])
    total = mine[1] * jnp.exp(mine[0] - top) + other[1] * jnp.exp(other[0] - top)
    return mine[2] + other[2] - top - jnp.log(total)


def conv_kernel(x_ref, rim_ref, weight_ref, bias_ref, proj_ref, conv_ref, out_ref, pad):
    rows = x_ref.shape[0]
    taps = weight_ref.shape[0]
    x = x_ref[...].astype(F32)
    pad[8 : 8 + rows, :] = x
    pad[8 - (taps - 1) : 8, :] = rim_ref[...].astype(F32)
    conv = bias_ref[...]
    for tap in range(taps):
        start = 8 - (taps - 1) + tap
        conv = conv + weight_ref[tap : tap + 1, :] * pad[start : start + rows, :]
    value = (conv / (1.0 + jnp.exp(-conv))).astype(BF16)
    conv_ref[...] = value
    part = lax.dot_general(value, proj_ref[...], (((1,), (1,)), ((), ())), preferred_element_type=F32)

    @pl.when(pl.program_id(0) == 0)
    def _():
        out_ref[...] = part

    @pl.when(pl.program_id(0) > 0)
    def _():
        out_ref[...] += part


def convolve(mamba_in, rim, conv_weight, conv_bias, x_proj):
    rows, channels = mamba_in.shape
    taps = conv_weight.shape[0]
    width = x_proj.shape[0]
    block = 1024
    return pl.pallas_call(
        conv_kernel,
        grid=(channels // block,),
        in_specs=[
            pl.BlockSpec((rows, block), lambda i: (0, i)),
            pl.BlockSpec((taps - 1, block), lambda i: (0, i)),
            pl.BlockSpec((taps, block), lambda i: (0, i)),
            pl.BlockSpec((1, block), lambda i: (0, i)),
            pl.BlockSpec((width, block), lambda i: (0, i)),
        ],
        out_specs=[
            pl.BlockSpec((rows, block), lambda i: (0, i)),
            pl.BlockSpec((rows, width), lambda i: (0, 0)),
        ],
        out_shape=[
            jax.ShapeDtypeStruct((rows, channels), BF16),
            jax.ShapeDtypeStruct((rows, width), F32),
        ],
        scratch_shapes=[pltpu.VMEM((rows + 8, block), F32)],
        compiler_params=params(60),
        cost_estimate=cost(rows * channels * 700, rows * channels * 4, rows * channels * 2),
        name="convolution",
    )(mamba_in, rim, conv_weight, conv_bias.reshape(1, channels), x_proj)


def softplus(v):
    e = jnp.exp(-jnp.abs(v))
    return jnp.maximum(v, 0.0) + jnp.log1p(e)


def spread(table, wide_s, rows):
    for n in range(table.shape[1]):
        wide_s[n * rows : (n + 1) * rows, :] = jnp.broadcast_to(table[:, n : n + 1], (rows, LANES))


def scan_kernel(
    mine_ref, other_ref, dt_ref, bias_ref, alog_ref, skip_ref, conv_ref, after_ref,
    y_ref, cum_ref, message_ref, delta_s, x_s, wide_s, rate_s,
):
    rows, rank = mine_ref.shape[0], dt_ref.shape[0]
    nstate = alog_ref.shape[0]

    @pl.when(pl.program_id(0) == 0)
    def _():
        spread(mine_ref[:, rank:] + other_ref[:, rank:], wide_s, rows)

    low = (mine_ref[:, :rank] + other_ref[:, :rank]).astype(BF16)
    for sub in range(8):
        at = slice(sub * LANES, (sub + 1) * LANES)
        product = jnp.dot(low, dt_ref[:, at], preferred_element_type=F32)
        delta_s[:, sub, :] = softplus(product + bias_ref[:, at])
        x_s[:, sub, :] = conv_ref[:, at].astype(F32)
    for n in range(nstate):
        rate_s[n] = -LOG2E * jnp.exp(alog_ref[n])

    def step(block, carry):
        cum, state = carry
        start = block * TOKENS
        ds = [delta_s[start + k] for k in range(TOKENS)]
        xs = [x_s[start + k] for k in range(TOKENS)]
        cums, ys = [], []
        for k in range(TOKENS):
            cum = cum + ds[k]
            dx = ds[k] * xs[k]
            sums = [skip_ref[...] * xs[k], jnp.zeros_like(cum)]
            new = []
            for n in range(nstate):
                row = n * rows + start + k
                h = jnp.exp2(ds[k] * rate_s[n]) * state[n] + dx * wide_s[pl.ds(row, 1), :]
                sums[n % 2] = sums[n % 2] + h * wide_s[pl.ds(row + nstate * rows, 1), :]
                new.append(h)
            state = tuple(new)
            cums.append(cum)
            ys.append(sums[0] + sums[1])
        for k in range(TOKENS):
            cum_ref[start + k] = cums[k]
            y_ref[start + k] = ys[k]
        return cum, state

    zero = jnp.zeros((8, LANES), F32)
    cum, state = lax.fori_loop(0, rows // TOKENS, step, (zero, (zero,) * nstate))
    high = cum.astype(BF16).astype(F32)
    message_ref[0] = jnp.concatenate(state + (high, cum - high), axis=0).astype(BF16)


def local_scan(mine, other, dt_proj, dt_bias, a_log, d_skip, conv_out, after):
    rows, channels = conv_out.shape
    rank = dt_proj.shape[0]
    nstate = a_log.shape[0]
    subs = channels // LANES
    folded = pl.BlockSpec((rows, 8, LANES), lambda i: (0, i, 0))
    states = pl.BlockSpec((nstate, 8, LANES), lambda i: (0, i, 0))
    whole = pl.BlockSpec(mine.shape, lambda i: (0, 0))
    return pl.pallas_call(
        scan_kernel,
        grid=(channels // GROUP,),
        in_specs=[
            whole,
            whole,
            pl.BlockSpec((rank, GROUP), lambda i: (0, i)),
            pl.BlockSpec((1, GROUP), lambda i: (0, i)),
            states,
            pl.BlockSpec((8, LANES), lambda i: (i, 0)),
            pl.BlockSpec((rows, GROUP), lambda i: (0, i)),
            pl.BlockSpec(memory_space=pl.ANY),
        ],
        out_specs=[folded, folded, pl.BlockSpec((1, 8 * (nstate + 2), LANES), lambda i: (i, 0, 0))],
        out_shape=[
            jax.ShapeDtypeStruct((rows, subs, LANES), F32),
            jax.ShapeDtypeStruct((rows, subs, LANES), F32),
            jax.ShapeDtypeStruct((channels // GROUP, 8 * (nstate + 2), LANES), BF16),
        ],
        scratch_shapes=[
            pltpu.VMEM((rows, 8, LANES), F32),
            pltpu.VMEM((rows, 8, LANES), F32),
            pltpu.VMEM((rows * nstate * 2, LANES), F32),
            pltpu.VMEM((nstate, 8, LANES), F32),
        ],
        compiler_params=params(62),
        cost_estimate=cost(rows * channels * nstate * 1600, rows * channels * 12, rows * channels * nstate),
        name="local_scan",
    )(
        mine, other, dt_proj, dt_bias.reshape(1, channels), a_log, d_skip.reshape(subs, LANES),
        conv_out, after,
    )


def finish_kernel(y_ref, cum_ref, mine_ref, other_ref, state_ref, alog_ref, gate_ref, out_ref, y_s, wide_s, rate_s):
    rows = y_ref.shape[0]
    nstate = alog_ref.shape[0]
    start = mine_ref.shape[1] - nstate

    @pl.when(pl.program_id(0) == 0)
    def _():
        spread(mine_ref[:, start:] + other_ref[:, start:], wide_s, rows)

    for n in range(nstate):
        rate_s[n] = -LOG2E * jnp.exp(alog_ref[n])

    def step(block, carry):
        start = block * TOKENS
        cums = [cum_ref[start + k] for k in range(TOKENS)]
        ys = [[y_ref[start + k], jnp.zeros((8, LANES), F32)] for k in range(TOKENS)]
        for n in range(nstate):
            rate, state = rate_s[n], state_ref[0, 8 * n : 8 * n + 8, :]
            for k in range(TOKENS):
                term = (jnp.exp2(cums[k] * rate) * state) * wide_s[pl.ds(n * rows + start + k, 1), :]
                ys[k][n % 2] = ys[k][n % 2] + term
        for k in range(TOKENS):
            y_s[start + k] = ys[k][0] + ys[k][1]
        return carry

    lax.fori_loop(0, rows // TOKENS, step, 0)
    for sub in range(8):
        at = slice(sub * LANES, (sub + 1) * LANES)
        half = 0.5 * gate_ref[:, at].astype(F32)
        out_ref[:, at] = (y_s[:, sub, :] * (half * jnp.tanh(half) + half)).astype(BF16)


def finish(y, cum, mine, other, incoming, a_log, mamba_gate):
    rows, channels = mamba_gate.shape
    nstate = a_log.shape[0]
    folded = pl.BlockSpec((rows, 8, LANES), lambda i: (0, i, 0))
    states = pl.BlockSpec((nstate, 8, LANES), lambda i: (0, i, 0))
    whole = pl.BlockSpec(mine.shape, lambda i: (0, 0))
    return pl.pallas_call(
        finish_kernel,
        grid=(channels // GROUP,),
        in_specs=[
            folded,
            folded,
            whole,
            whole,
            pl.BlockSpec((1, 8 * nstate, LANES), lambda i: (i, 0, 0)),
            states,
            pl.BlockSpec((rows, GROUP), lambda i: (0, i)),
        ],
        out_specs=pl.BlockSpec((rows, GROUP), lambda i: (0, i)),
        out_shape=jax.ShapeDtypeStruct((rows, channels), BF16),
        scratch_shapes=[
            pltpu.VMEM((rows, 8, LANES), F32),
            pltpu.VMEM((rows * nstate, LANES), F32),
            pltpu.VMEM((nstate, 8, LANES), F32),
        ],
        compiler_params=params(48),
        cost_estimate=cost(rows * channels * nstate * 1000, rows * channels * 12, rows * channels * nstate),
        name="finish",
    )(y, cum, mine, other, incoming, a_log, mamba_gate)


def join_kernel(size, first, last, place_ref, alog_ref, *refs):
    came, refs = refs[:size], refs[size:]
    if not first:
        old_sum_ref, old_ref, refs = refs[0], refs[1], refs[2:]
    nstate = alog_ref.shape[0]
    mine = place_ref[0]
    groups = came[0].shape[0]
    for g in range(groups):
        at = slice(8 * g, 8 * g + 8)
        ordered = []
        for j in range(size):
            pick = mine ^ j
            chosen = came[0][g]
            for k in range(1, size):
                chosen = jnp.where(pick == k, came[k][g], chosen)
            ordered.append(chosen.astype(F32))
        row = lambda j, n: ordered[j][8 * n : 8 * n + 8, :]
        added = [row(j, nstate) + row(j, nstate + 1) for j in range(size)]
        zero = jnp.zeros((8, LANES), F32)
        running, prefix = added[0], zero
        for j in range(1, size):
            prefix = jnp.where(mine == j, running, prefix)
            running = running + added[j]
        total_rows = []
        for n in range(nstate):
            rate = -LOG2E * jnp.exp(alog_ref[n, at, :])
            state, before = row(0, n), zero
            for j in range(1, size):
                before = jnp.where(mine == j, state, before)
                if j < size - 1 or not last:
                    state = state * jnp.exp2(rate * added[j]) + row(j, n)
            if not first:
                before = before * jnp.exp2(rate * old_sum_ref[g]) + old_ref[g, 8 * n : 8 * n + 8, :]
            refs[0][g, 8 * n : 8 * n + 8, :] = before
            total_rows.append(state)
        if not last:
            refs[1][g] = prefix if first else prefix + old_sum_ref[g]
            high = running.astype(BF16).astype(F32)
            refs[2][g] = jnp.concatenate(total_rows + [high, running - high], axis=0).astype(BF16)


def joined(message, a_log, beside):
    nstate = a_log.shape[0]
    groups = message.shape[0]
    place = lax.axis_index("seq")
    count = lax.axis_size("seq")
    smem = pl.BlockSpec(memory_space=pltpu.SMEM)
    vmem = pl.BlockSpec(memory_space=pltpu.VMEM)
    stride = 1
    old = []
    results = []
    sizes = (4, 2, 4, 4)
    for stage, (size, work) in enumerate(zip(sizes, beside)):
        first, last = stage == 0, stage == len(sizes) - 1
        mine = ((place // stride) % size).astype(jnp.int32).reshape(1)
        came = [message]
        for k in range(1, size):
            pairs = [(i, i ^ (k * stride)) for i in range(count)]
            came.append(lax.ppermute(message, "seq", pairs))
        done = [piece(message) for piece in work]
        if done:
            came, done = lax.optimization_barrier((came, done))
        results.extend(done)
        shapes = [jax.ShapeDtypeStruct((groups, 8 * nstate, LANES), F32)]
        if not last:
            shapes += [jax.ShapeDtypeStruct((groups, 8, LANES), F32), jax.ShapeDtypeStruct(message.shape, BF16)]
        outs = pl.pallas_call(
            functools.partial(join_kernel, size, first, last),
            in_specs=[smem] + [vmem] * (1 + size + len(old)),
            out_specs=[vmem] * len(shapes),
            out_shape=shapes,
            compiler_params=params(24),
            cost_estimate=cost(1e8, message.size * 2 * size, message.size * size),
            name="join",
        )(mine, a_log, *came, *old)
        if not last:
            old = [outs[1], outs[0]]
            message = outs[2]
        stride *= size
    return outs[0], results


def payload_kernel(turn_ref, own_ref, z1_ref, z2_ref, *outs):
    for step, out_ref in enumerate(outs, 1):
        out_ref[0] = z1_ref[...]
        wraps = turn_ref[0] + step >= 4

        @pl.when(wraps)
        def _():
            out_ref[1] = z2_ref[...]

        @pl.when(jnp.logical_not(wraps))
        def _():
            out_ref[1] = own_ref[...]


def payloads(turn, own, z1, z2):
    smem = pl.BlockSpec(memory_space=pltpu.SMEM)
    vmem = pl.BlockSpec(memory_space=pltpu.VMEM)
    return pl.pallas_call(
        payload_kernel,
        in_specs=[smem, vmem, vmem, vmem],
        out_specs=[vmem] * 3,
        out_shape=[jax.ShapeDtypeStruct((2,) + own.shape, BF16)] * 3,
        compiler_params=params(32),
        cost_estimate=cost(0, own.size * 18, 0),
        name="payload",
    )(turn, own, z1, z2)


def prepare_kernel(first_ref, turn_ref, own_ref, z1_ref, z2_ref, r1_ref, r2_ref, r3_ref, key_ref, value_ref):
    rows = own_ref.shape[1]
    local_kv = own_ref.shape[0] // (2 * HEAD_DIM)
    tiles = WINDOW // rows + 1
    first = first_ref[0]
    turn = turn_ref[0]
    pad = LANES - HEAD_DIM
    line = lax.broadcasted_iota(jnp.int32, (pad, rows), 0)
    empty = jnp.zeros((rows, pad), BF16)
    moved = (None, r1_ref, r2_ref, r3_ref)
    for tile in range(tiles):
        at = slice(tile * rows, (tile + 1) * rows)
        if tile % 4 == 0:
            block = (z2_ref, z1_ref, own_ref)[tile // 4][...]
        else:
            step = 4 - tile % 4
            early = tile < 4
            block = moved[step][jnp.where((turn < step) == early, 1, 0)]
        extra = jnp.where(line == 0, jnp.where(tile < first, LOW, 0.0), 0.0).astype(BF16)
        for head in range(local_kv):
            key = block[head * HEAD_DIM : (head + 1) * HEAD_DIM, :]
            value = block[(local_kv + head) * HEAD_DIM : (local_kv + head + 1) * HEAD_DIM, :]
            key_ref[head, :, at] = jnp.concatenate((key, extra), axis=0)
            turned = jnp.transpose(value.astype(F32)).astype(BF16)
            value_ref[head, at, :] = jnp.concatenate((turned, empty), axis=1)


def prepare(first, turn, own, z1, z2, moved):
    rows = own.shape[1]
    local_kv = own.shape[0] // (2 * HEAD_DIM)
    span = WINDOW + rows
    smem = pl.BlockSpec(memory_space=pltpu.SMEM)
    vmem = pl.BlockSpec(memory_space=pltpu.VMEM)
    return pl.pallas_call(
        prepare_kernel,
        in_specs=[smem, smem] + [vmem] * 6,
        out_specs=[vmem, vmem],
        out_shape=[
            jax.ShapeDtypeStruct((local_kv, LANES, span), BF16),
            jax.ShapeDtypeStruct((local_kv, span, LANES), BF16),
        ],
        compiler_params=params(32),
        cost_estimate=cost(1e9, own.size * 18, 0),
        name="prepare",
    )(first, turn, own, z1, z2, *moved)


def attention_kernel(q_ref, key_ref, value_ref, after_ref, out_ref, score_a, score_b):
    rows, width = q_ref.shape
    span = key_ref.shape[2]
    tiles = span // rows
    heads = width // HEAD_DIM
    lane = lax.broadcasted_iota(jnp.int32, (rows, LANES - HEAD_DIM), 1)
    one = jnp.where(lane == 0, 1.0, 0.0).astype(BF16)
    qpos = lax.broadcasted_iota(jnp.int32, (rows, rows), 0)
    cpos = lax.broadcasted_iota(jnp.int32, (rows, rows), 1)
    factor = HEAD_DIM ** (-0.5) * LOG2E
    store = (score_a, score_b)

    def query_of(head):
        return jnp.concatenate((q_ref[:, head * HEAD_DIM : (head + 1) * HEAD_DIM], one), axis=1)

    def scored(query, head, tile, top):
        at = slice(tile * rows, (tile + 1) * rows)
        score = jnp.dot(query, key_ref[0, :, at], preferred_element_type=F32)
        if tile == 0:
            score = jnp.where(cpos > qpos, score, -jnp.inf)
        if tile == tiles - 1:
            score = jnp.where(cpos <= qpos, score, -jnp.inf)
        store[head % 2][:, at] = score
        for piece in range(rows // LANES):
            top = jnp.maximum(top, score[:, piece * LANES : (piece + 1) * LANES])
        return top

    low = jnp.full((rows, LANES), -jnp.inf, F32)
    top = low
    query = query_of(0)
    for tile in range(tiles):
        top = scored(query, 0, tile, top)
    for head in range(heads):
        best = jnp.max(top, axis=1, keepdims=True)
        total = jnp.zeros((rows, LANES), F32)
        mixed = jnp.zeros((rows, LANES), F32)
        top = low
        if head + 1 < heads:
            query = query_of(head + 1)
        for tile in range(tiles):
            at = slice(tile * rows, (tile + 1) * rows)
            if head + 1 < heads:
                top = scored(query, head + 1, tile, top)
            prob = jnp.exp2((store[head % 2][:, at] - best) * factor)
            for piece in range(rows // LANES):
                total = total + prob[:, piece * LANES : (piece + 1) * LANES]
            mixed = mixed + jnp.dot(prob.astype(BF16), value_ref[0, at, :], preferred_element_type=F32)
        result = mixed / jnp.sum(total, axis=1, keepdims=True)
        out_ref[:, head * HEAD_DIM : (head + 1) * HEAD_DIM] = result[:, :HEAD_DIM].astype(BF16)


def attention_piece(queries, key, value, piece, after):
    rows = queries.shape[0]
    local_kv, _, span = key.shape
    heads = queries.shape[1] // HEAD_DIM
    share = heads // PIECES
    kv = piece * share // (heads // local_kv)
    pairs = rows * span * share
    return pl.pallas_call(
        attention_kernel,
        grid=(1,),
        in_specs=[
            pl.BlockSpec((rows, share * HEAD_DIM), lambda i: (0, piece)),
            pl.BlockSpec((1, LANES, span), lambda i: (kv, 0, 0)),
            pl.BlockSpec((1, span, LANES), lambda i: (kv, 0, 0)),
            pl.BlockSpec(memory_space=pl.ANY),
        ],
        out_specs=pl.BlockSpec((rows, share * HEAD_DIM), lambda i: (0, 0)),
        out_shape=jax.ShapeDtypeStruct((rows, share * HEAD_DIM), BF16),
        scratch_shapes=[pltpu.VMEM((rows, span), F32), pltpu.VMEM((rows, span), F32)],
        compiler_params=params(48),
        cost_estimate=cost(pairs * 2600, rows * 4096, pairs),
        name="attention",
    )(queries, key, value, after)


def local(
    mamba_in, mamba_gate, conv_weight, conv_bias, x_proj, dt_proj, dt_bias, a_log, d_skip,
    queries, keys, att_values, logits, targets, allowed,
):
    rows, channels = mamba_in.shape
    taps = conv_weight.shape[0]
    nstate = a_log.shape[0]
    subs = channels // LANES
    place = lax.axis_index("seq")
    count = lax.axis_size("seq")
    rim = shifted(mamba_in[rows - (taps - 1) :], "seq", 1)
    own = jnp.concatenate((keys.T, att_values.T), axis=0)
    z1 = shifted(own, "seq", 4)
    z2 = shifted(own, "seq", 8)
    first = jnp.maximum(WINDOW // rows - place, 0).astype(jnp.int32).reshape(1)
    turn = (place % 4).astype(jnp.int32).reshape(1)
    sent = payloads(turn, own, z1, z2)
    moved = []
    for step, payload in enumerate(sent, 1):
        pairs = [(i, i - i % 4 + (i + step) % 4) for i in range(count)]
        moved.append(lax.ppermute(payload, "seq", pairs))
    conv_out, part = convolve(mamba_in, rim, conv_weight, conv_bias, x_proj.T)
    other = swapped(part)
    folded = a_log.reshape(nstate, subs, LANES)
    y, cum, message = local_scan(part, other, dt_proj, dt_bias, folded, d_skip, conv_out, sent[2])
    made = {}

    def score(message):
        return scoring_part(logits, targets, allowed, [message] + moved)

    def attend(piece):
        def run(message):
            if not made:
                made["kv"] = prepare(first, turn, own, z1, z2, moved)
            return attention_piece(queries, *made["kv"], piece, message)

        return run

    incoming, results = joined(message, folded, [[score], [attend(0)], [attend(1), attend(2)], [attend(3)]])
    stats = results[0]
    attention_out = jnp.concatenate(results[1:], axis=1)
    loglik = scoring_join(stats, swapped(stats))
    mamba_out = finish(y, cum, part, other, incoming, folded, mamba_gate)
    return (mamba_out, attention_out, loglik)


def solution(mesh):
    in_specs = (
        P("seq", "vocab"),
        P("seq", "vocab"),
        P(None, "vocab"),
        P("vocab"),
        P("vocab", None),
        P(None, "vocab"),
        P("vocab"),
        P(None, "vocab"),
        P("vocab"),
        P("seq", "vocab"),
        P("seq", "vocab"),
        P("seq", "vocab"),
        P("seq", "vocab"),
        P("seq"),
        P("seq", "vocab"),
    )
    out_specs = (P("seq", "vocab"), P("seq", "vocab"), P("seq"))
    return jax.shard_map(local, mesh=mesh, in_specs=in_specs, out_specs=out_specs, check_vma=False)
```

time: 150 us -> 129 us (0.86)
  local copies, waits for them, and re-layouts: 14.5 us -> 4.01 us
  Pallas kernels: 75.1 us -> 70.9 us
  waiting for transfers between devices: 15.3 us -> 11.9 us
  other arithmetic: 5.49 us -> 2.92 us
    unnamed x42 -> x29, local copies, waits for them, and re-layouts: 9.96 us -> 3.01 us
    pallas_call x2 -> x11, Pallas kernels: 47.4 us -> 42.2 us  [the longest x1 24.3 us: local_scan(): pl.pallas_call(scan_kernel, grid=(channels // GROUP,), in_specs=[whole, w...]
    ppermute x13, waiting for transfers between devices: 15.3 us -> 11.9 us  [the longest x10 11.9 us: joined(): came.append(lax.ppermute(message, 'seq', pairs))]
    broadcast_in_dim x4 -> x0, local copies, waits for them, and re-layouts: 2.8 us -> none  [the longest x2 2.1 us: local(): jnp.broadcast_to(proj[:, rank + nstate:].reshape(rows * nstate, 1), (rows...]
    pallas_call x1, Pallas kernels: 16.5 us -> 14.1 us  [finish(): pl.pallas_call(finish_kernel, grid=(channels // GROUP,), in_specs=[folded...]
    pallas_call x1, Pallas kernels: 6.68 us -> 8.46 us  [scoring_part(): pl.pallas_call(score_kernel, grid=(rows // block,), in_specs=[pl.BlockSpe...]
    concatenate x5 -> x2, other arithmetic: 0.19 us -> 1.9 us  [the longest x1 0.96 us: local(): own = jnp.concatenate((keys.T, att_values.T), axis=0)]
    ppermute x13, starting transfers between devices: 22 us -> 23.7 us  [the longest x10 18.2 us: joined(): came.append(lax.ppermute(message, 'seq', pairs))]
  transfers between devices with their start and end apart: 18 -> 18, of which waited for: 8 -> 4; matrix products, arithmetic and copies ran while one was open for 9% -> 2% of each run, Pallas kernels for 40% -> 41%
where the time goes in v2:
time: 129 us; the launch traced here: 128 us
  Pallas kernels  70.9 us (55%)
  starting transfers between devices  37.5 us (29%)
  waiting for transfers between devices  11.9 us (9%)
  local copies, waits for them, and re-layouts  4.01 us (3%)
  other arithmetic  2.92 us (2%)
    pallas_call x1, Pallas kernels, local_scan(): pl.pallas_call(scan_kernel, grid=(channels // GROUP,), in_specs=[whole, w...  24.3 us
    ppermute x10, starting transfers between devices, joined(): came.append(lax.ppermute(message, 'seq', pairs))  18.2 us
    pallas_call x4, Pallas kernels, attention_piece(): pl.pallas_call(attention_kernel, grid=(1,), in_specs=[pl.BlockSpec((rows,...  14.4 us
    pallas_call x1, Pallas kernels, finish(): pl.pallas_call(finish_kernel, grid=(channels // GROUP,), in_specs=[folded...  14.1 us
    ppermute x3, starting transfers between devices, shifted(): lax.ppermute(value, axis, [(source, source + steps) for source in range(l...  13.7 us
    ppermute x10, waiting for transfers between devices, joined(): came.append(lax.ppermute(message, 'seq', pairs))  11.9 us
    pallas_call x1, Pallas kernels, scoring_part(): pl.pallas_call(score_kernel, grid=(rows // block,), in_specs=[pl.BlockSpe...  8.46 us
    pallas_call x1, Pallas kernels, convolve(): pl.pallas_call(conv_kernel, grid=(channels // block,), in_specs=[pl.Block...  6.13 us
  transfers between devices with their start and end apart: 18, of which 4 were waited for; matrix products, arithmetic and copies ran while one was open for 2% of the time, Pallas kernels for 41%

profile of v2, /device:TPU:32, one launch (start us, length us, event | category | flops | bytes accessed | tf_op | source)
XLA Modules:
  0.0 128.3 jit_solution(10734027898152941203)
XLA Ops:
  0.6 0.8 slice.26
  1.4 3.5 %collective-permute-start = (bf16[3,3072]{1,0:T(4,128)(2,1)S(1)}, bf16[3,3072]{1,0:T(4,128)(2,1)S(1)}, u32[]{:S(2)}, u32[]{:S(2)}) collective-permute-start(bf16[3,3072]{1,0:T(4,128)(2,1)S(1)} %slice.26), channel_id=1, source_target_pairs={{0,2},{2,4},{4,6},{6,8},{8,10},{10,12},{12,14},{14,16},{16,18},{18... | collective-permute-start | bytes 55304 | tf_op jit(solution)/shard_map/ppermute | solution.py:35
  4.9 1.0 pad_maximum_fusion.1.own_ref
  5.9 3.8 %collective-permute-start.2 = (bf16[384,256]{1,0:T(8,128)(2,1)S(1)}, bf16[384,256]{1,0:T(8,128)(2,1)S(1)}, u32[]{:S(2)}, u32[]{:S(2)}) collective-permute-start(bf16[384,256]{1,0:T(8,128)(2,1)S(1)} %pad_maximum_fusion.1.own_ref), channel_id=1, source_target_pairs={{0,8},{2,10},{4,12},{6,14},{8,16},{10,18},{12,20},{14,22},{16,24},... | collective-permute-start | bytes 589832 | tf_op jit(solution)/shard_map/ppermute | solution.py:35
  9.7 6.4 %collective-permute-start.3 = (bf16[384,256]{1,0:T(8,128)(2,1)S(1)}, bf16[384,256]{1,0:T(8,128)(2,1)S(1)}, u32[]{:S(2)}, u32[]{:S(2)}) collective-permute-start(bf16[384,256]{1,0:T(8,128)(2,1)S(1)} %pad_maximum_fusion.1.own_ref), channel_id=1, source_target_pairs={{0,16},{2,18},{4,20},{6,22},{8,24},{10,26},{12,28},{14,30},{16,32}... | collective-permute-start | bytes 589832 | tf_op jit(solution)/shard_map/ppermute | solution.py:35
  16.2 0.0 copy-start.12
  16.2 0.6 copy-done.12
  16.8 6.1 %convolution.1 = (bf16[256,3072]{1,0:T(8,128)(2,1)}, f32[256,224]{1,0:T(8,128)}) custom-call(bf16[256,3072]{1,0:T(8,128)(2,1)} %x_ref.1, bf16[3,3072]{1,0:T(4,128)(2,1)} %copy-done.12, f32[4,3072]{1,0:T(4,128)} %weight_ref.1, f32[1,3072]{1,0:T(1,128)} %bitcast.26, bf16[224,3072]{1,0:T(8,128)(2,1)} %bitcast.22), custom_call_target="tpu_custom_call" | custom-call | flops 550502400 | bytes 3145728 | tf_op jit(solution)/shard_map/convolution/pallas_call | solution.py:135
  23.0 0.7 copy.19
  23.7 0.1 copy.18.local_target_ref
  23.9 0.0 collective-permute-done.3.z2_ref
  23.9 1.1 payload.1
  25.0 1.6 %collective-permute-start.7 = (bf16[2,384,256]{2,1,0:T(8,128)(2,1)}, bf16[2,384,256]{2,1,0:T(8,128)(2,1)S(1)}, u32[]{:S(2)}, u32[]{:S(2)}) collective-permute-start(bf16[2,384,256]{2,1,0:T(8,128)(2,1)} %get-tuple-element.47), channel_id=1, source_target_pairs={{0,2},{2,4},{4,6},{6,0},{8,10},{10,12},{12,14},{14,8},{16,18},{18,... | collective-permute-start | bytes 1179656 | tf_op jit(solution)/shard_map/ppermute | solution.py:578
  26.6 2.0 %collective-permute-start.8 = (bf16[2,384,256]{2,1,0:T(8,128)(2,1)}, bf16[2,384,256]{2,1,0:T(8,128)(2,1)}, u32[]{:S(2)}, u32[]{:S(2)}) collective-permute-start(bf16[2,384,256]{2,1,0:T(8,128)(2,1)} %get-tuple-element.48), channel_id=1, source_target_pairs={{0,4},{2,6},{4,0},{6,2},{8,12},{10,14},{12,8},{14,10},{16,20},{18,... | collective-permute-start | bytes 1179656 | tf_op jit(solution)/shard_map/ppermute | solution.py:578
  28.6 2.0 %collective-permute-start.9 = (bf16[2,384,256]{2,1,0:T(8,128)(2,1)}, bf16[2,384,256]{2,1,0:T(8,128)(2,1)}, u32[]{:S(2)}, u32[]{:S(2)}) collective-permute-start(bf16[2,384,256]{2,1,0:T(8,128)(2,1)} %get-tuple-element.43.after_ref), channel_id=1, source_target_pairs={{0,6},{2,0},{4,2},{6,4},{8,14},{10,8},{12,10},{14,12},{16,22},{18,... | collective-permute-start | bytes 1179656 | tf_op jit(solution)/shard_map/ppermute | solution.py:578
  30.6 0.0 collective-permute-done.1.other_ref
  30.6 0.7 copy-done.8
  31.3 24.3 %local_scan.1 = (f32[256,24,128]{2,1,0:T(8,128)}, f32[256,24,128]{2,1,0:T(8,128)}, bf16[3,144,128]{2,1,0:T(8,128)(2,1)}) custom-call(f32[256,224]{1,0:T(8,128)} %get-tuple-element.41.mine_ref, f32[256,224]{1,0:T(8,128)} %copy-done.8, bf16[192,3072]{1,0:T(8,128)(2,1)} %dt_ref.1, f32[1,3072]{1,0:T(1,128)} %bitcast.28, f32[16,24,128]{2,1,0:T(8,128)} %bitcast.16, ...), custom_call_target="tpu_custom_call" | custom-call | flops 20132659200 | bytes 9437184 | tf_op jit(solution)/shard_map/local_scan/pallas_call | solution.py:228
  55.6 0.2 collective-permute-start.4
  55.7 1.5 %collective-permute-start.5 = (bf16[3,144,128]{2,1,0:T(8,128)(2,1)}, bf16[3,144,128]{2,1,0:T(8,128)(2,1)S(1)}, u32[]{:S(2)}, u32[]{:S(2)}) collective-permute-start(bf16[3,144,128]{2,1,0:T(8,128)(2,1)} %get-tuple-element.49.refs_0_), channel_id=1, source_target_pairs={{0,4},{2,6},{4,0},{6,2},{8,12},{10,14},{12,8},{14,10},{16,20},{18,... | collective-permute-start | bytes 331784 | tf_op jit(solution)/shard_map/ppermute | solution.py:383
  57.3 3.1 %collective-permute-start.6 = (bf16[3,144,128]{2,1,0:T(8,128)(2,1)}, bf16[3,144,128]{2,1,0:T(8,128)(2,1)S(1)}, u32[]{:S(2)}, u32[]{:S(2)}) collective-permute-start(bf16[3,144,128]{2,1,0:T(8,128)(2,1)} %get-tuple-element.49.refs_0_), channel_id=1, source_target_pairs={{0,6},{2,4},{4,2},{6,0},{8,14},{10,12},{12,10},{14,8},{16,22},{18,... | collective-permute-start | bytes 331784 | tf_op jit(solution)/shard_map/ppermute | solution.py:383
  60.4 0.9 copy-done.2
  61.3 8.5 %scoring.1 = f32[256,128]{1,0:T(8,128)S(1)} custom-call(bf16[256,8192]{1,0:T(8,128)(2,1)} %logits_ref.1, s32[256,1024]{1,0:T(8,128)S(1)} %copy-done.1, s32[256,1]{1,0:T(8,128)S(1)} %copy.18.local_target_ref, bf16[3,144,128]{2,1,0:T(8,128)(2,1)S(1)} %copy-done.2, bf16[2,384,256]{2,1,0:T(8,128)(2,1)S(1)} %collective-permute-done.7.refs_1_.r1_ref, ...), custom_call_target="tpu_custom_call" | custom-call | flops 536870912 | bytes 6291456 | tf_op jit(solution)/shard_map/scoring/pallas_call | solution.py:83
  69.8 0.1 collective-permute-start.17
  70.0 0.3 join.4
  70.2 0.3 collective-permute-start.10
  70.5 0.0 copy-start.6
  70.5 1.6 %prepare.1 = (bf16[2,128,2304]{2,1,0:T(8,128)(2,1)S(1)}, bf16[2,2304,128]{2,1,0:T(8,128)(2,1)S(1)}) custom-call(s32[1]{0:T(128)} %bitcast.12.first_ref, s32[1]{0:T(128)} %bitcast.4.turn_ref.place_ref, bf16[384,256]{1,0:T(8,128)(2,1)S(1)} %pad_maximum_fusion.1.own_ref, bf16[384,256]{1,0:T(8,128)(2,1)S(1)} %collective-permute-done.2.z1_ref, ...), custom_call_target="tpu_custom_call" | custom-call | flops 1000000000 | bytes 1769472 | tf_op jit(solution)/shard_map/prepare/pallas_call | solution.py:468
  72.2 3.6 %attention.4 = bf16[256,384]{1,0:T(8,128)(2,1)S(1)} custom-call(bf16[256,1536]{1,0:T(8,128)(2,1)S(1)} %copy-done.6, bf16[2,128,2304]{2,1,0:T(8,128)(2,1)S(1)} %get-tuple-element.54.key_ref, bf16[2,2304,128]{2,1,0:T(8,128)(2,1)S(1)} %get-tuple-element.55.value_ref, bf16[3,144,128]{2,1,0:T(8,128)(2,1)S(1)} %get-tuple-element.56.after_ref.refs_0_), custom_call_target="tpu_custom_call" | custom-call | flops 6134169600 | bytes 1048576 | tf_op jit(solution)/shard_map/attention/pallas_call | solution.py:540
  75.8 0.4 fusion
  76.2 0.6 log_subtract_fusion
  76.8 0.1 join.5
  76.9 3.6 %attention.6 = bf16[256,384]{1,0:T(8,128)(2,1)S(1)} custom-call(bf16[256,1536]{1,0:T(8,128)(2,1)S(1)} %copy-done.6, bf16[2,128,2304]{2,1,0:T(8,128)(2,1)S(1)} %get-tuple-element.54.key_ref, bf16[2,2304,128]{2,1,0:T(8,128)(2,1)S(1)} %get-tuple-element.55.value_ref, bf16[3,144,128]{2,1,0:T(8,128)(2,1)S(1)} %get-tuple-element.61.after_ref.refs_0_), custom_call_target="tpu_custom_call" | custom-call | flops 6134169600 | bytes 1048576 | tf_op jit(solution)/shard_map/attention/pallas_call | solution.py:540
  80.5 2.7 %collective-permute-start.11 = (bf16[3,144,128]{2,1,0:T(8,128)(2,1)S(1)}, bf16[3,144,128]{2,1,0:T(8,128)(2,1)S(1)}, u32[]{:S(2)}, u32[]{:S(2)}) collective-permute-start(bf16[3,144,128]{2,1,0:T(8,128)(2,1)S(1)} %get-tuple-element.61.after_ref.refs_0_), channel_id=1, source_target_pairs={{0,16},{2,18},{4,20},{6,22},{8,24},{10,26},{12,28},{14,30},{16,0},... | collective-permute-start | bytes 331784 | tf_op jit(solution)/shard_map/ppermute | solution.py:383
  83.2 4.3 %collective-permute-start.12 = (bf16[3,144,128]{2,1,0:T(8,128)(2,1)S(1)}, bf16[3,144,128]{2,1,0:T(8,128)(2,1)S(1)}, u32[]{:S(2)}, u32[]{:S(2)}) collective-permute-start(bf16[3,144,128]{2,1,0:T(8,128)(2,1)S(1)} %get-tuple-element.61.after_ref.refs_0_), channel_id=1, source_target_pairs={{0,32},{2,34},{4,36},{6,38},{8,40},{10,42},{12,44},{14,46},{16,48}... | collective-permute-start | bytes 331784 | tf_op jit(solution)/shard_map/ppermute | solution.py:383
  87.4 0.3 collective-permute-start.13
  87.7 3.6 %attention.5 = bf16[256,384]{1,0:T(8,128)(2,1)S(1)} custom-call(bf16[256,1536]{1,0:T(8,128)(2,1)S(1)} %copy-done.6, bf16[2,128,2304]{2,1,0:T(8,128)(2,1)S(1)} %get-tuple-element.54.key_ref, bf16[2,2304,128]{2,1,0:T(8,128)(2,1)S(1)} %get-tuple-element.55.value_ref, bf16[3,144,128]{2,1,0:T(8,128)(2,1)S(1)} %get-tuple-element.61.after_ref.refs_0_), custom_call_target="tpu_custom_call" | custom-call | flops 6134169600 | bytes 1048576 | tf_op jit(solution)/shard_map/attention/pallas_call | solution.py:540
  91.3 1.0 collective-permute-done.12.refs_2_
  92.4 7.1 %collective-permute-done.13.refs_3_ = bf16[3,144,128]{2,1,0:T(8,128)(2,1)S(1)} collective-permute-done((bf16[3,144,128]{2,1,0:T(8,128)(2,1)S(1)}, bf16[3,144,128]{2,1,0:T(8,128)(2,1)S(1)}, u32[]{:S(2)}, u32[]{:S(2)}) %collective-permute-start.13) | collective-permute-done | bytes 110624 | tf_op jit(solution)/shard_map/ppermute | solution.py:383
  99.4 0.3 join.6
  99.7 2.9 %collective-permute-start.14 = (bf16[3,144,128]{2,1,0:T(8,128)(2,1)S(1)}, bf16[3,144,128]{2,1,0:T(8,128)(2,1)S(1)}, u32[]{:S(2)}, u32[]{:S(2)}) collective-permute-start(bf16[3,144,128]{2,1,0:T(8,128)(2,1)S(1)} %get-tuple-element.68.after_ref.refs_0_), channel_id=1, source_target_pairs={{0,64},{2,66},{4,68},{6,70},{8,72},{10,74},{12,76},{14,78},{16,80}... | collective-permute-start | bytes 331784 | tf_op jit(solution)/shard_map/ppermute | solution.py:383
  102.6 3.0 %collective-permute-start.15 = (bf16[3,144,128]{2,1,0:T(8,128)(2,1)S(1)}, bf16[3,144,128]{2,1,0:T(8,128)(2,1)S(1)}, u32[]{:S(2)}, u32[]{:S(2)}) collective-permute-start(bf16[3,144,128]{2,1,0:T(8,128)(2,1)S(1)} %get-tuple-element.68.after_ref.refs_0_), channel_id=1, source_target_pairs={{0,128},{2,130},{4,132},{6,134},{8,136},{10,138},{12,140},{14,142}... | collective-permute-start | bytes 331784 | tf_op jit(solution)/shard_map/ppermute | solution.py:383
  105.6 3.6 %attention.7 = bf16[256,384]{1,0:T(8,128)(2,1)S(1)} custom-call(bf16[256,1536]{1,0:T(8,128)(2,1)S(1)} %copy-done.6, bf16[2,128,2304]{2,1,0:T(8,128)(2,1)S(1)} %get-tuple-element.54.key_ref, bf16[2,2304,128]{2,1,0:T(8,128)(2,1)S(1)} %get-tuple-element.55.value_ref, bf16[3,144,128]{2,1,0:T(8,128)(2,1)S(1)} %get-tuple-element.68.after_ref.refs_0_), custom_call_target="tpu_custom_call" | custom-call | flops 6134169600 | bytes 1048576 | tf_op jit(solution)/shard_map/attention/pallas_call | solution.py:540
  109.2 1.8 %collective-permute-done.15.refs_2_ = bf16[3,144,128]{2,1,0:T(8,128)(2,1)S(1)} collective-permute-done((bf16[3,144,128]{2,1,0:T(8,128)(2,1)S(1)}, bf16[3,144,128]{2,1,0:T(8,128)(2,1)S(1)}, u32[]{:S(2)}, u32[]{:S(2)}) %collective-permute-start.15) | collective-permute-done | bytes 110624 | tf_op jit(solution)/shard_map/ppermute | solution.py:383
  111.0 2.0 %collective-permute-done.16.refs_3_ = bf16[3,144,128]{2,1,0:T(8,128)(2,1)S(1)} collective-permute-done((bf16[3,144,128]{2,1,0:T(8,128)(2,1)S(1)}, bf16[3,144,128]{2,1,0:T(8,128)(2,1)S(1)}, u32[]{:S(2)}, u32[]{:S(2)}) %collective-permute-start.16) | collective-permute-done | bytes 110624 | tf_op jit(solution)/shard_map/ppermute | solution.py:383
  113.0 0.9 pad_maximum_fusion
  113.9 0.2 join.7.state_ref
  114.2 14.1 %finish.1 = bf16[256,3072]{1,0:T(8,128)(2,1)} custom-call(f32[256,24,128]{2,1,0:T(8,128)S(1)} %copy-done.10, f32[256,24,128]{2,1,0:T(8,128)} %get-tuple-element.45.cum_ref, f32[256,224]{1,0:T(8,128)S(1)} %copy-done.7, f32[256,224]{1,0:T(8,128)S(1)} %copy-done.9, f32[3,128,128]{2,1,0:T(8,128)S(1)} %join.7.state_ref, f32[16,24,128]{2,1,0:T(8,128)S(1)} %bitcast.21, ...), custom_call_target="tpu_custom_call" | custom-call | flops 12582912000 | bytes 9437184 | tf_op jit(solution)/shard_map/finish/pallas_call | solution.py:300
  (39 shorter events, 0.1 us)
Async XLA Ops:
  1.4 14.7 %collective-permute-start = (bf16[3,3072]{1,0:T(4,128)(2,1)S(1)}, bf16[3,3072]{1,0:T(4,128)(2,1)S(1)}, u32[]{:S(2)}, u32[]{:S(2)}) collective-permute-start(bf16[3,3072]{1,0:T(4,128)(2,1)S(1)} %slice.26), channel_id=1, source_target_pairs={{0,2},{2,4},{4,6},{6,8},{8,10},{10,12},{12,14},{14,16},{16,18},{18... | collective-permute-start | bytes 55304 | tf_op jit(solution)/shard_map/ppermute | solution.py:35
  5.9 18.0 %collective-permute-start.2 = (bf16[384,256]{1,0:T(8,128)(2,1)S(1)}, bf16[384,256]{1,0:T(8,128)(2,1)S(1)}, u32[]{:S(2)}, u32[]{:S(2)}) collective-permute-start(bf16[384,256]{1,0:T(8,128)(2,1)S(1)} %pad_maximum_fusion.1.own_ref), channel_id=1, source_target_pairs={{0,8},{2,10},{4,12},{6,14},{8,16},{10,18},{12,20},{14,22},{16,24},... | collective-permute-start | bytes 589832 | tf_op jit(solution)/shard_map/ppermute | solution.py:35
  9.7 14.2 %collective-permute-start.3 = (bf16[384,256]{1,0:T(8,128)(2,1)S(1)}, bf16[384,256]{1,0:T(8,128)(2,1)S(1)}, u32[]{:S(2)}, u32[]{:S(2)}) collective-permute-start(bf16[384,256]{1,0:T(8,128)(2,1)S(1)} %pad_maximum_fusion.1.own_ref), channel_id=1, source_target_pairs={{0,16},{2,18},{4,20},{6,22},{8,24},{10,26},{12,28},{14,30},{16,32}... | collective-permute-start | bytes 589832 | tf_op jit(solution)/shard_map/ppermute | solution.py:35
  16.2 0.6 copy-start.12
  16.8 6.2 %copy-start.11 = (f32[16,3072]{1,0:T(8,128)S(1)}, f32[16,3072]{1,0:T(8,128)}, u32[]{:S(2)}) copy-start(f32[16,3072]{1,0:T(8,128)} %param.22) | copy-start | bytes 589828
  16.8 7.0 %copy-start.13 = (s32[256]{0:T(256)S(1)}, s32[256]{0:T(256)}, u32[]{:S(2)}) copy-start(s32[256]{0:T(256)} %param.28) | copy-start | bytes 3076
  22.9 7.7 %collective-permute-start.1 = (f32[256,224]{1,0:T(8,128)}, f32[256,224]{1,0:T(8,128)S(1)}, u32[]{:S(2)}, u32[]{:S(2)}) collective-permute-start(f32[256,224]{1,0:T(8,128)} %get-tuple-element.41.mine_ref), channel_id=1, source_target_pairs={{0,1},{1,0},{2,3},{3,2},{4,5},{5,4},{6,7},{7,6},{8,9},{9,8},{10,11... | collective-permute-start | bytes 688136 | tf_op jit(solution)/shard_map/ppermute | solution.py:39
  23.9 1.1 copy-start.3
  25.0 32.2 %collective-permute-start.7 = (bf16[2,384,256]{2,1,0:T(8,128)(2,1)}, bf16[2,384,256]{2,1,0:T(8,128)(2,1)S(1)}, u32[]{:S(2)}, u32[]{:S(2)}) collective-permute-start(bf16[2,384,256]{2,1,0:T(8,128)(2,1)} %get-tuple-element.47), channel_id=1, source_target_pairs={{0,2},{2,4},{4,6},{6,0},{8,10},{10,12},{12,14},{14,8},{16,18},{18,... | collective-permute-start | bytes 1179656 | tf_op jit(solution)/shard_map/ppermute | solution.py:578
  26.6 33.8 %collective-permute-start.8 = (bf16[2,384,256]{2,1,0:T(8,128)(2,1)}, bf16[2,384,256]{2,1,0:T(8,128)(2,1)}, u32[]{:S(2)}, u32[]{:S(2)}) collective-permute-start(bf16[2,384,256]{2,1,0:T(8,128)(2,1)} %get-tuple-element.48), channel_id=1, source_target_pairs={{0,4},{2,6},{4,0},{6,2},{8,12},{10,14},{12,8},{14,10},{16,20},{18,... | collective-permute-start | bytes 1179656 | tf_op jit(solution)/shard_map/ppermute | solution.py:578
  28.6 31.8 %collective-permute-start.9 = (bf16[2,384,256]{2,1,0:T(8,128)(2,1)}, bf16[2,384,256]{2,1,0:T(8,128)(2,1)}, u32[]{:S(2)}, u32[]{:S(2)}) collective-permute-start(bf16[2,384,256]{2,1,0:T(8,128)(2,1)} %get-tuple-element.43.after_ref), channel_id=1, source_target_pairs={{0,6},{2,0},{4,2},{6,4},{8,14},{10,8},{12,10},{14,12},{16,22},{18,... | collective-permute-start | bytes 1179656 | tf_op jit(solution)/shard_map/ppermute | solution.py:578
  30.6 0.7 copy-start.8
  31.3 29.1 %copy-start.1 = (s32[256,1024]{1,0:T(8,128)S(1)}, s32[256,1024]{1,0:T(8,128)}, u32[]{:S(2)}) copy-start(s32[256,1024]{1,0:T(8,128)} %allowed_ref.1) | copy-start | bytes 3145732
  55.6 14.4 %copy-start = (f32[2,8,24,128]{3,2,1,0:T(8,128)S(1)}, f32[2,8,24,128]{3,2,1,0:T(8,128)}, u32[]{:S(2)}) copy-start(f32[2,8,24,128]{3,2,1,0:T(8,128)} %copy.19) | copy-start | bytes 589828
  55.6 14.2 %collective-permute-start.4 = (bf16[3,144,128]{2,1,0:T(8,128)(2,1)}, bf16[3,144,128]{2,1,0:T(8,128)(2,1)S(1)}, u32[]{:S(2)}, u32[]{:S(2)}) collective-permute-start(bf16[3,144,128]{2,1,0:T(8,128)(2,1)} %get-tuple-element.49.refs_0_), channel_id=1, source_target_pairs={{0,2},{2,0},{4,6},{6,4},{8,10},{10,8},{12,14},{14,12},{16,18},{18,... | collective-permute-start | bytes 331784 | tf_op jit(solution)/shard_map/ppermute | solution.py:383
  55.7 14.1 %collective-permute-start.5 = (bf16[3,144,128]{2,1,0:T(8,128)(2,1)}, bf16[3,144,128]{2,1,0:T(8,128)(2,1)S(1)}, u32[]{:S(2)}, u32[]{:S(2)}) collective-permute-start(bf16[3,144,128]{2,1,0:T(8,128)(2,1)} %get-tuple-element.49.refs_0_), channel_id=1, source_target_pairs={{0,4},{2,6},{4,0},{6,2},{8,12},{10,14},{12,8},{14,10},{16,20},{18,... | collective-permute-start | bytes 331784 | tf_op jit(solution)/shard_map/ppermute | solution.py:383
  57.3 12.6 %collective-permute-start.6 = (bf16[3,144,128]{2,1,0:T(8,128)(2,1)}, bf16[3,144,128]{2,1,0:T(8,128)(2,1)S(1)}, u32[]{:S(2)}, u32[]{:S(2)}) collective-permute-start(bf16[3,144,128]{2,1,0:T(8,128)(2,1)} %get-tuple-element.49.refs_0_), channel_id=1, source_target_pairs={{0,6},{2,4},{4,2},{6,0},{8,14},{10,12},{12,10},{14,8},{16,22},{18,... | collective-permute-start | bytes 331784 | tf_op jit(solution)/shard_map/ppermute | solution.py:383
  60.4 0.9 copy-start.2
  61.3 9.2 %copy-start.4 = (bf16[384,256]{1,0:T(8,128)(2,1)S(1)}, bf16[384,256]{1,0:T(8,128)(2,1)}, u32[]{:S(2)}) copy-start(bf16[384,256]{1,0:T(8,128)(2,1)} %copy-done.3) | copy-start | bytes 589828
  69.8 5.9 %collective-permute-start.17 = (f32[8,256]{0,1:T(8,128)S(1)}, f32[8,256]{0,1:T(8,128)S(1)}, u32[]{:S(2)}, u32[]{:S(2)}) collective-permute-start(f32[8,256]{0,1:T(8,128)S(1)} %slice_bitcast_fusion), channel_id=1, source_target_pairs={{0,1},{1,0},{2,3},{3,2},{4,5},{5,4},{6,7},{7,6},{8,9},{9,8},{10,11... | collective-permute-start | bytes 24584 | tf_op jit(solution)/shard_map/ppermute | solution.py:39
  70.2 6.6 %collective-permute-start.10 = (bf16[3,144,128]{2,1,0:T(8,128)(2,1)S(1)}, bf16[3,144,128]{2,1,0:T(8,128)(2,1)S(1)}, u32[]{:S(2)}, u32[]{:S(2)}) collective-permute-start(bf16[3,144,128]{2,1,0:T(8,128)(2,1)S(1)} %get-tuple-element.56.after_ref.refs_0_), channel_id=1, source_target_pairs={{0,8},{2,10},{4,12},{6,14},{8,0},{10,2},{12,4},{14,6},{16,24},{18,... | collective-permute-start | bytes 331784 | tf_op jit(solution)/shard_map/ppermute | solution.py:383
  70.5 1.6 %copy-start.6 = (bf16[256,1536]{1,0:T(8,128)(2,1)S(1)}, bf16[256,1536]{1,0:T(8,128)(2,1)}, u32[]{:S(2)}) copy-start(bf16[256,1536]{1,0:T(8,128)(2,1)} %q_ref.7) | copy-start | bytes 2359300
  80.5 10.8 %collective-permute-start.11 = (bf16[3,144,128]{2,1,0:T(8,128)(2,1)S(1)}, bf16[3,144,128]{2,1,0:T(8,128)(2,1)S(1)}, u32[]{:S(2)}, u32[]{:S(2)}) collective-permute-start(bf16[3,144,128]{2,1,0:T(8,128)(2,1)S(1)} %get-tuple-element.61.after_ref.refs_0_), channel_id=1, source_target_pairs={{0,16},{2,18},{4,20},{6,22},{8,24},{10,26},{12,28},{14,30},{16,0},... | collective-permute-start | bytes 331784 | tf_op jit(solution)/shard_map/ppermute | solution.py:383
  83.2 9.2 %collective-permute-start.12 = (bf16[3,144,128]{2,1,0:T(8,128)(2,1)S(1)}, bf16[3,144,128]{2,1,0:T(8,128)(2,1)S(1)}, u32[]{:S(2)}, u32[]{:S(2)}) collective-permute-start(bf16[3,144,128]{2,1,0:T(8,128)(2,1)S(1)} %get-tuple-element.61.after_ref.refs_0_), channel_id=1, source_target_pairs={{0,32},{2,34},{4,36},{6,38},{8,40},{10,42},{12,44},{14,46},{16,48}... | collective-permute-start | bytes 331784 | tf_op jit(solution)/shard_map/ppermute | solution.py:383
  87.4 12.0 %collective-permute-start.13 = (bf16[3,144,128]{2,1,0:T(8,128)(2,1)S(1)}, bf16[3,144,128]{2,1,0:T(8,128)(2,1)S(1)}, u32[]{:S(2)}, u32[]{:S(2)}) collective-permute-start(bf16[3,144,128]{2,1,0:T(8,128)(2,1)S(1)} %get-tuple-element.61.after_ref.refs_0_), channel_id=1, source_target_pairs={{0,48},{2,50},{4,52},{6,54},{8,56},{10,58},{12,60},{14,62},{16,32}... | collective-permute-start | bytes 331784 | tf_op jit(solution)/shard_map/ppermute | solution.py:383
  99.7 9.5 %collective-permute-start.14 = (bf16[3,144,128]{2,1,0:T(8,128)(2,1)S(1)}, bf16[3,144,128]{2,1,0:T(8,128)(2,1)S(1)}, u32[]{:S(2)}, u32[]{:S(2)}) collective-permute-start(bf16[3,144,128]{2,1,0:T(8,128)(2,1)S(1)} %get-tuple-element.68.after_ref.refs_0_), channel_id=1, source_target_pairs={{0,64},{2,66},{4,68},{6,70},{8,72},{10,74},{12,76},{14,78},{16,80}... | collective-permute-start | bytes 331784 | tf_op jit(solution)/shard_map/ppermute | solution.py:383
  102.6 8.4 %collective-permute-start.15 = (bf16[3,144,128]{2,1,0:T(8,128)(2,1)S(1)}, bf16[3,144,128]{2,1,0:T(8,128)(2,1)S(1)}, u32[]{:S(2)}, u32[]{:S(2)}) collective-permute-start(bf16[3,144,128]{2,1,0:T(8,128)(2,1)S(1)} %get-tuple-element.68.after_ref.refs_0_), channel_id=1, source_target_pairs={{0,128},{2,130},{4,132},{6,134},{8,136},{10,138},{12,140},{14,142}... | collective-permute-start | bytes 331784 | tf_op jit(solution)/shard_map/ppermute | solution.py:383
  105.6 7.4 %collective-permute-start.16 = (bf16[3,144,128]{2,1,0:T(8,128)(2,1)S(1)}, bf16[3,144,128]{2,1,0:T(8,128)(2,1)S(1)}, u32[]{:S(2)}, u32[]{:S(2)}) collective-permute-start(bf16[3,144,128]{2,1,0:T(8,128)(2,1)S(1)} %get-tuple-element.68.after_ref.refs_0_), channel_id=1, source_target_pairs={{0,192},{2,194},{4,196},{6,198},{8,200},{10,202},{12,204},{14,206}... | collective-permute-start | bytes 331784 | tf_op jit(solution)/shard_map/ppermute | solution.py:383
  105.6 8.6 %copy-start.10 = (f32[256,24,128]{2,1,0:T(8,128)S(1)}, f32[256,24,128]{2,1,0:T(8,128)}, u32[]{:S(2)}) copy-start(f32[256,24,128]{2,1,0:T(8,128)} %get-tuple-element.44.y_ref) | copy-start | bytes 9437188
  109.2 5.0 %copy-start.5 = (bf16[256,3072]{1,0:T(8,128)(2,1)S(1)}, bf16[256,3072]{1,0:T(8,128)(2,1)}, u32[]{:S(2)}) copy-start(bf16[256,3072]{1,0:T(8,128)(2,1)} %gate_ref.1) | copy-start | bytes 4718596
  109.2 5.0 %copy-start.7 = (f32[256,224]{1,0:T(8,128)S(1)}, f32[256,224]{1,0:T(8,128)}, u32[]{:S(2)}) copy-start(f32[256,224]{1,0:T(8,128)} %get-tuple-element.41.mine_ref) | copy-start | bytes 688132
  109.2 5.0 %copy-start.9 = (f32[256,224]{1,0:T(8,128)S(1)}, f32[256,224]{1,0:T(8,128)}, u32[]{:S(2)}) copy-start(f32[256,224]{1,0:T(8,128)} %copy-done.8) | copy-start | bytes 688132
